TPU v7x, 128 devices: a whole 4x4x4 slice. The times are simulated.
128 devices in a mesh: dp: 32 (over z, x, core), tensor: 4 (over y).
Axes of the slice: x: 4, y: 4, z: 4, core: 2. Of those that a mesh axis runs over, the one named last changes fastest.
Arguments:
- tokens: bfloat16 [32768, 1024], P(('dp', 'tensor')), may hold values from -6 to 6
- cotangent: bfloat16 [32768, 1024], P(('dp', 'tensor')), may hold values from -6 to 6
- gain_attn: float32 [1024], replicated, may hold values from 0.5 to 1.5
- w_query: bfloat16 [1024, 1024], P(None, 'tensor'), may hold values from -0.1875 to 0.1875
- key_projection_weight: bfloat16 [1024, 512], P(None, 'tensor'), may hold values from -0.1875 to 0.1875
- value_projection_weight: bfloat16 [1024, 512], P(None, 'tensor'), may hold values from -0.1875 to 0.1875
- w_out: bfloat16 [1024, 1024], P('tensor'), may hold values from -1.5 to 1.5
- gain_moe: float32 [1024], replicated, may hold values from 0.5 to 1.5
- w_router: bfloat16 [1024, 32], replicated, may hold values from -0.09375 to 0.09375
- w_gate: bfloat16 [32, 1024, 512], P('dp', None, 'tensor'), may hold values from -0.1875 to 0.1875
- w_up: bfloat16 [32, 1024, 512], P('dp', None, 'tensor'), may hold values from -0.1875 to 0.1875
- w_down: bfloat16 [32, 512, 1024], P('dp', 'tensor'), may hold values from -1.5 to 1.5
- routes: int32 [32768, 8], P(('dp', 'tensor')), may hold values from 0 to 31, all different within a row; in each aligned block of 256 rows (0 to 255, 256 to 511, ...) at most 96 rows name the same one
- owner_map: int32 [32], replicated, may hold values from 0 to 31, each once
Outputs:
- mixed_out: bfloat16 [32768, 1024], P(('dp', 'tensor'))
- d_tokens: float32 [32768, 1024], P(('dp', 'tensor'))
- g_gain_attn: float32 [1024], replicated
- g_query: float32 [1024, 1024], P(None, 'tensor')
- g_key: float32 [1024, 512], P(None, 'tensor')
- g_value: float32 [1024, 512], P(None, 'tensor')
- g_out: float32 [1024, 1024], P('tensor')
- g_gain_moe: float32 [1024], replicated
- g_router: float32 [1024, 32], replicated
- g_gate: float32 [32, 1024, 512], P('dp', None, 'tensor')
- g_up: float32 [32, 1024, 512], P('dp', None, 'tensor')
- g_down: float32 [32, 512, 1024], P('dp', 'tensor')
Inputs may be any that keep to these rules, and one draw needn't show every extreme that they name: `routes`: each row names 8 different experts. Within the rows of one device no expert is named more than 96 times, and in some devices' rows one expert is named exactly 96 times. Each value once: expert e uses slot owner_map[e] of w_gate, w_up and w_down.
All inputs are finite; a program needn't handle non-finite values.
Results may differ from a plain program's by a relative error of at most 0.025.
Values may be sent and summed in bfloat16 or wider, within the bound.
No kernel may reach another device: no remote copies, remote signals or barrier semaphores. Data moves between devices by JAX's collectives and lax.ppermute only.
A program may use at most 192 MiB of HBM per device.

v0:
```python
import math

import jax
import jax.numpy as jnp
from jax import lax
from jax.sharding import PartitionSpec as P

HEAD_DIM = 64
SEQUENCE_LENGTH = 1024


norm_eps = 1e-05


def from_everyone(array, axis):
    copies = jnp.broadcast_to(array, (lax.axis_size(axis), *array.shape))
    return lax.all_to_all(copies, axis, split_axis=0, concat_axis=0, tiled=True)


def in_order(blocks, dim):
    lengths = list(blocks.shape[1:])
    lengths[dim] *= blocks.shape[0]
    return jnp.moveaxis(blocks, 0, dim).reshape(lengths)


def gathered_copies(array, axis, dim):
    blocks = from_everyone(array, axis)
    return in_order(blocks, dim)


def cut_along(array, dim, count):
    before, after = (array.shape[:dim], array.shape[dim + 1 :])
    return jnp.moveaxis(array.reshape(*before, count, -1, *after), dim, 0)


def summed_on_arrival(array, axis, dim):
    count = lax.axis_size(axis)
    blocks = lax.all_to_all(cut_along(array, dim, count), axis, 0, 0, tiled=True)
    return jnp.sum(blocks.astype(jnp.float32), axis=0)


def gather_turned(arrays, axis, dims):
    turned = [jnp.moveaxis(a, dim, 0) for a, dim in zip(arrays, dims)]
    widths = [t[0].size for t in turned]
    both = jnp.concatenate([t.reshape(-1, w) for t, w in zip(turned, widths)], axis=1)
    result = lax.all_gather(both, axis, axis=0, tiled=True)
    blocks = jnp.split(result, [sum(widths[:k]) for k in range(1, len(widths))], axis=1)
    return tuple(
        (
            jnp.moveaxis(b.reshape(-1, *t.shape[1:]), 0, dim)
            for b, t, dim in zip(blocks, turned, dims)
        )
    )


def in_one_piece(arrays, axis, dim, along):
    ends, at = ([], 0)
    for a in arrays[:-1]:
        at += a.shape[along]
        ends.append(at)
    both = jnp.concatenate(arrays, axis=along)
    return tuple(
        jnp.split(lax.psum_scatter(both, axis, scatter_dimension=dim, tiled=True), ends, axis=along)
    )


def rms_norm(values, gain_vec):
    return (
        values * lax.rsqrt(jnp.mean(values * values, axis=-1, keepdims=True) + norm_eps) * gain_vec
    )


def rotary_embedding(values, seq_length):
    row_count, head_count, head_size = values.shape
    half_size = head_size // 2
    steps_f = jnp.arange(half_size).astype(values.dtype)
    inv_freq = jnp.exp(steps_f * (-2.0 * math.log(10000.0) / head_size))
    positions = (jnp.arange(row_count) % seq_length).astype(values.dtype)
    angles = positions[:, None] * inv_freq[None, :]
    cosine = jnp.concatenate([jnp.cos(angles), jnp.cos(angles)], axis=1)[:, None, :]
    sine = jnp.concatenate([jnp.sin(angles), jnp.sin(angles)], axis=1)[:, None, :]
    turned = jnp.concatenate([-values[..., half_size:], values[..., :half_size]], axis=-1)
    return values * cosine + turned * sine


def cross_rows(left_rows, right_rows):
    return jnp.einsum("nd,nf->df", left_rows, right_rows, preferred_element_type=jnp.float32)


def shards(
    tokens,
    cotangent,
    gain_attn,
    w_query,
    key_projection_weight,
    value_projection_weight,
    w_out,
    gain_moe,
    w_router,
    w_gate,
    w_up,
    w_down,
    routes,
    owner_map,
):
    tensor_count = lax.axis_size("tensor")
    dp_count = lax.axis_size("dp")
    local_rows = tokens.shape[0]
    model_width = tokens.shape[1]
    group_rows = local_rows * tensor_count
    head_size = HEAD_DIM
    query_heads = w_query.shape[1] // head_size
    kv_heads = key_projection_weight.shape[1] // head_size
    group_size = query_heads // kv_heads
    seq_length = SEQUENCE_LENGTH
    block_rows = min(512, seq_length)
    blocks_per = seq_length // block_rows
    block_total = group_rows // block_rows
    score_scale = head_size ** (-0.5)
    resid = tokens.astype(jnp.float32)
    attention_normed_input, norm_a_pull = jax.vjp(rms_norm, resid, gain_attn)
    gathered = gathered_copies(attention_normed_input.astype(jnp.bfloat16), "tensor", 0)
    query_pre = jnp.dot(gathered, w_query, preferred_element_type=jnp.float32).reshape(
        group_rows, query_heads, head_size
    )
    key_pre = jnp.dot(gathered, key_projection_weight, preferred_element_type=jnp.float32).reshape(
        group_rows, kv_heads, head_size
    )
    query_rot, query_pull = jax.vjp(lambda values: rotary_embedding(values, seq_length), query_pre)
    key_rot, key_pull = jax.vjp(lambda values: rotary_embedding(values, seq_length), key_pre)
    query_low = query_rot.astype(jnp.bfloat16).reshape(group_rows, kv_heads, group_size, head_size)
    key_low = key_rot.astype(jnp.bfloat16)
    value_low = (
        jnp.dot(gathered, value_projection_weight, preferred_element_type=jnp.float32)
        .astype(jnp.bfloat16)
        .reshape(group_rows, kv_heads, head_size)
    )

    def block_inputs(block_id):
        seq_start = block_id // blocks_per * seq_length
        first_row = seq_start + block_id % blocks_per * block_rows
        query_block = lax.dynamic_slice_in_dim(query_low, first_row, block_rows, 0)
        raw_scores = jnp.einsum(
            "qhgd,khd->hgqk", query_block, key_low, preferred_element_type=jnp.float32
        )
        query_pos = first_row - seq_start + jnp.arange(block_rows)
        causal = jnp.arange(seq_length)[None, :] <= query_pos[:, None]
        masked = jnp.where(causal, raw_scores * score_scale, -jnp.inf)
        return (first_row, query_block, key_low, value_low, masked)

    def forward_block(block_id):
        first_row, query_block, key_seq, value_seq, masked = block_inputs(block_id)
        row_peak = jnp.max(masked, axis=-1, keepdims=True)
        log_total = row_peak + jnp.log(jnp.sum(jnp.exp(masked - row_peak), axis=-1, keepdims=True))
        probs_low = jnp.exp(masked - log_total).astype(jnp.bfloat16)
        mixed_heads = jnp.einsum(
            "hgqk,khd->qhgd", probs_low, value_seq, preferred_element_type=jnp.float32
        )
        return (mixed_heads.astype(jnp.bfloat16), log_total)

    block_ids = jnp.arange(block_total, dtype=jnp.int32)
    attn_blocks, log_totals = lax.map(forward_block, block_ids)
    attention_output = attn_blocks.reshape(group_rows, query_heads * head_size)
    hidden = resid + summed_on_arrival(
        jnp.dot(attention_output, w_out, preferred_element_type=jnp.float32).astype(jnp.bfloat16),
        "tensor",
        0,
    )
    normed_m, norm_m_pull = jax.vjp(rms_norm, hidden, gain_moe)
    normed_m_low = normed_m.astype(jnp.bfloat16)
    logits = jnp.dot(normed_m_low, w_router, preferred_element_type=jnp.float32)
    expert_count = owner_map.shape[0]
    top_count = routes.shape[1]
    route_picks = routes[:, :, None] == jnp.arange(expert_count, dtype=jnp.int32)[None, None, :]
    chosen = jnp.sum(jnp.where(route_picks, logits[:, None, :], 0.0), axis=-1)
    route_gates = jax.nn.softmax(chosen, axis=-1)
    route_slots = jnp.sum(jnp.where(route_picks, owner_map[None, None, :], 0), axis=-1).reshape(-1)
    route_total = local_rows * top_count
    capacity = local_rows * 3 // 8
    slots_local = expert_count // dp_count
    slot_hits = route_slots[:, None] == jnp.arange(expert_count, dtype=jnp.int32)[None, :]
    slot_ranks = jnp.cumsum(slot_hits.astype(jnp.int32), axis=0) - 1
    positions = jnp.sum(jnp.where(slot_hits, slot_ranks, 0), axis=1)
    destination = route_slots * capacity + positions
    filled = (
        jnp.full((expert_count * capacity,), route_total, jnp.int32)
        .at[destination]
        .set(jnp.arange(route_total, dtype=jnp.int32))
    )
    source_token = filled // top_count
    padded_rows = jnp.concatenate([normed_m_low, jnp.zeros((1, model_width), jnp.bfloat16)], axis=0)
    send_rows = padded_rows[source_token].reshape(dp_count, slots_local, capacity, model_width)
    gate_w, up_w, down_w = gather_turned((w_gate, w_up, w_down), "tensor", (2, 2, 1))
    expert_in = lax.all_to_all(send_rows, "dp", split_axis=0, concat_axis=0, tiled=True)
    gate_part = jnp.einsum("secd,edf->secf", expert_in, gate_w, preferred_element_type=jnp.float32)
    up_part = jnp.einsum("secd,edf->secf", expert_in, up_w, preferred_element_type=jnp.float32)
    act_part = (gate_part * jax.nn.sigmoid(gate_part) * up_part).astype(jnp.bfloat16)
    out_rows_low = jnp.einsum(
        "secf,efd->secd", act_part, down_w, preferred_element_type=jnp.float32
    ).astype(jnp.bfloat16)
    returned = lax.all_to_all(out_rows_low, "dp", split_axis=0, concat_axis=0, tiled=True)
    sigmoid_gate = jax.nn.sigmoid(gate_part)
    silu_gate = gate_part * sigmoid_gate
    routed = returned.reshape(expert_count * capacity, model_width)[destination].reshape(
        local_rows, top_count, model_width
    )
    routed_f = routed.astype(jnp.float32)
    mixed_out = (hidden + jnp.einsum("tk,tkd->td", route_gates, routed_f)).astype(jnp.bfloat16)
    grad_top = cotangent.astype(jnp.float32)
    d_route = jnp.einsum("tkd,td->tk", routed_f, grad_top)
    d_chosen = route_gates * (d_route - jnp.sum(route_gates * d_route, axis=-1, keepdims=True))
    d_logits = jnp.sum(jnp.where(route_picks, d_chosen[:, :, None], 0.0), axis=1).astype(
        jnp.bfloat16
    )
    router_part = cross_rows(normed_m_low, d_logits)
    d_normed_m = jnp.dot(d_logits, w_router.T, preferred_element_type=jnp.float32)
    d_expert = (
        (route_gates[:, :, None] * grad_top[:, None, :])
        .astype(jnp.bfloat16)
        .reshape(route_total, model_width)
    )
    d_padded = jnp.concatenate([d_expert, jnp.zeros((1, model_width), jnp.bfloat16)], axis=0)
    send_grads = d_padded[filled].reshape(dp_count, slots_local, capacity, model_width)
    grad_in = lax.all_to_all(send_grads, "dp", split_axis=0, concat_axis=0, tiled=True)
    d_act = jnp.einsum("secd,efd->secf", grad_in, down_w, preferred_element_type=jnp.float32)
    d_up_low = (d_act * silu_gate).astype(jnp.bfloat16)
    d_gate_low = (d_act * up_part * sigmoid_gate * (1.0 + gate_part * (1.0 - sigmoid_gate))).astype(
        jnp.bfloat16
    )
    grad_down = jnp.einsum("secf,secd->efd", act_part, grad_in, preferred_element_type=jnp.float32)
    grad_gate = jnp.einsum(
        "secd,secf->edf", expert_in, d_gate_low, preferred_element_type=jnp.float32
    )
    grad_up = jnp.einsum("secd,secf->edf", expert_in, d_up_low, preferred_element_type=jnp.float32)
    d_in_full = jnp.einsum("secf,edf->secd", d_gate_low, gate_w, preferred_element_type=jnp.float32)
    d_in_full = d_in_full + jnp.einsum(
        "secf,edf->secd", d_up_low, up_w, preferred_element_type=jnp.float32
    )
    grad_gate, grad_up, grad_down = (
        *tuple(
            (
                part.astype(jnp.float32)
                for part in in_one_piece(
                    (grad_gate.astype(jnp.bfloat16), grad_up.astype(jnp.bfloat16)), "tensor", 2, 0
                )
            )
        ),
        lax.psum_scatter(
            grad_down.astype(jnp.bfloat16), "tensor", scatter_dimension=1, tiled=True
        ).astype(jnp.float32),
    )
    grad_back = lax.all_to_all(
        d_in_full.astype(jnp.bfloat16), "dp", split_axis=0, concat_axis=0, tiled=True
    )
    d_routes_in = grad_back.reshape(expert_count * capacity, model_width)[destination].reshape(
        local_rows, top_count, model_width
    )
    d_normed_m = d_normed_m + jnp.sum(d_routes_in.astype(jnp.float32), axis=1)
    d_hidden_norm, gain_moe_part = norm_m_pull(d_normed_m)
    d_hidden = grad_top + d_hidden_norm
    grad_gathered = gathered_copies(d_hidden.astype(jnp.bfloat16), "tensor", 0)
    out_grad = cross_rows(attention_output, grad_gathered)
    d_attended = (
        jnp.dot(grad_gathered, w_out.T, preferred_element_type=jnp.float32)
        .astype(jnp.bfloat16)
        .reshape(group_rows, kv_heads, group_size, head_size)
    )

    def backward_block(block_pair):
        block_id, log_total = block_pair
        first_row, query_block, key_seq, value_seq, masked = block_inputs(block_id)
        attn_probs = jnp.exp(masked - log_total)
        probs_low = attn_probs.astype(jnp.bfloat16)
        grad_block = lax.dynamic_slice_in_dim(d_attended, first_row, block_rows, 0)
        d_probs = jnp.einsum(
            "qhgd,khd->hgqk", grad_block, value_seq, preferred_element_type=jnp.float32
        )
        row_delta = jnp.sum(attn_probs * d_probs, axis=-1, keepdims=True)
        d_raw = (attn_probs * (d_probs - row_delta) * score_scale).astype(jnp.bfloat16)
        d_query_blk = jnp.einsum(
            "hgqk,khd->qhgd", d_raw, key_seq, preferred_element_type=jnp.float32
        )
        d_key_blk = jnp.einsum(
            "hgqk,qhgd->khd", d_raw, query_block, preferred_element_type=jnp.float32
        )
        d_value_blk = jnp.einsum(
            "hgqk,qhgd->khd", probs_low, grad_block, preferred_element_type=jnp.float32
        )
        return (d_query_blk, d_key_blk, d_value_blk)

    d_query_all, d_key_all, d_value_all = lax.map(backward_block, (block_ids, log_totals))
    seq_count = group_rows // seq_length
    d_query_f = d_query_all.reshape(group_rows, query_heads, head_size)
    d_key_f = jnp.sum(
        d_key_all.reshape(seq_count, blocks_per, seq_length, kv_heads, head_size), axis=1
    ).reshape(group_rows, kv_heads, head_size)
    d_value_f = jnp.sum(
        d_value_all.reshape(seq_count, blocks_per, seq_length, kv_heads, head_size), axis=1
    ).reshape(group_rows, kv_heads * head_size)
    d_query_low = (
        query_pull(d_query_f)[0].reshape(group_rows, query_heads * head_size).astype(jnp.bfloat16)
    )
    d_key_low = key_pull(d_key_f)[0].reshape(group_rows, kv_heads * head_size).astype(jnp.bfloat16)
    d_value_low = d_value_f.astype(jnp.bfloat16)
    query_grad = cross_rows(gathered, d_query_low)
    key_grad = cross_rows(gathered, d_key_low)
    value_grad = cross_rows(gathered, d_value_low)
    summed = jnp.dot(d_query_low, w_query.T, preferred_element_type=jnp.float32)
    summed = summed + jnp.dot(
        d_key_low, key_projection_weight.T, preferred_element_type=jnp.float32
    )
    d_normed_a = summed_on_arrival(
        (
            summed
            + jnp.dot(d_value_low, value_projection_weight.T, preferred_element_type=jnp.float32)
        ).astype(jnp.bfloat16),
        "tensor",
        0,
    )
    d_resid_norm, gain_attn_part = norm_a_pull(d_normed_a)
    d_tokens = d_hidden + d_resid_norm
    g_query, g_key, g_value, g_out = (
        lax.psum(query_grad.astype(jnp.bfloat16), "dp").astype(jnp.float32),
        lax.psum(key_grad.astype(jnp.bfloat16), "dp").astype(jnp.float32),
        lax.psum(value_grad.astype(jnp.bfloat16), "dp").astype(jnp.float32),
        lax.psum(out_grad.astype(jnp.bfloat16), "dp").astype(jnp.float32),
    )
    g_gain_attn, g_gain_moe, g_router = lax.psum(
        (gain_attn_part, gain_moe_part, router_part), ("dp", "tensor")
    )
    return (
        mixed_out,
        d_tokens,
        g_gain_attn,
        g_query,
        g_key,
        g_value,
        g_out,
        g_gain_moe,
        g_router,
        grad_gate,
        grad_up,
        grad_down,
    )


def solution(mesh):
    in_specs = (
        P(("dp", "tensor"), None),
        P(("dp", "tensor"), None),
        P(),
        P(None, "tensor"),
        P(None, "tensor"),
        P(None, "tensor"),
        P("tensor", None),
        P(),
        P(),
        P("dp", None, "tensor"),
        P("dp", None, "tensor"),
        P("dp", "tensor", None),
        P(("dp", "tensor"), None),
        P(),
    )
    out_specs = (
        P(("dp", "tensor"), None),
        P(("dp", "tensor"), None),
        P(),
        P(None, "tensor"),
        P(None, "tensor"),
        P(None, "tensor"),
        P("tensor", None),
        P(),
        P(),
        P("dp", None, "tensor"),
        P("dp", None, "tensor"),
        P("dp", "tensor", None),
    )
    return jax.shard_map(shards, mesh=mesh, in_specs=in_specs, out_specs=out_specs, check_vma=False)
```

profile of v0, /device:TPU:14, one launch (start us, length us, event | category | flops | bytes accessed | tf_op | source)
XLA Modules:
  0.0 1012.2 jit_solution(1388302975561063498)
XLA Ops:
  19.9 22.4 %all-to-all-done = bf16[4,256,1024]{2,1,0:T(8,128)(2,1)S(1)} async-done(((bf16[4,256,1024]{2,1,0:T(8,128)(2,1)}), bf16[4,256,1024]{2,1,0:T(8,128)(2,1)S(1)}, u32[]{:S(2)}, u32[]{:S(2)}) %all-to-all-start) | async-done | bytes 2097184 | tf_op jit(solution)/shard_map/all_to_all | solution.py:17
  48.3 23.3 %while.30 = (s32[]{:T(128)}, bf16[2,512,2,2,64]{1,4,3,2,0:T(8,128)(2,1)}, f32[2,2,2,512,1]{3,2,1,4,0:T(2,128)S(1)}, s32[2]{0:T(128)S(1)}, bf16[1024,2,2,64]{0,3,...) while((s32[]{:T(128)}, ...), condition=%wide.region_4.5_spmd, body=%wide.region_1.4_spmd.sunk | while | flops 560593408 | bytes 32575952 | solution.py:162
  82.2 9.1 reduce-window.6
  92.4 8.3 scatter_custom_fusion
  108.4 14.0 %gather_fusion = bf16[3072,1024]{1,0:T(8,128)(2,1)} fusion(bf16[257,1024]{1,0:T(8,128)(2,1)S(1)} %concatenate.31, s32[3072]{0:T(1024)S(1)} %get-tuple-element.307), kind=kCustom, calls=%fused_computation | custom fusion | bytes 12595200 | tf_op jit(solution)/shard_map/gather | solution.py:192
  122.4 8.6 all-to-all-start.2
  132.2 44.6 %all-gather.2.cloned.1.call-done = bf16[512,3072]{0,1:T(8,128)(2,1)} async-done(((bf16[128,3072]{0,1:T(8,128)(2,1)}), bf16[512,3072]{0,1:T(8,128)(2,1)}) %all-gather.2.cloned.1.call-update) | async-done | bytes 3145744 | tf_op jit(solution)/shard_map/all_gather | solution.py:46
  176.8 27.9 %all-to-all-done.2 = bf16[32,1,96,1024]{3,2,1,0:T(8,128)(2,1)} async-done(((bf16[32,1,96,1024]{3,2,1,0:T(8,128)(2,1)}), bf16[32,1,96,1024]{3,2,1,0:T(8,128)(2,1)}, u32[]{:S(2)}, u32[]{:S(2)}) %all-to-all-start.2) | async-done | bytes 6291488 | tf_op jit(solution)/shard_map/all_to_all | solution.py:194
  210.7 7.8 fusion.90
  228.3 9.1 all-to-all-start.3
  238.9 72.3 %all-to-all-done.3 = bf16[32,1,96,1024]{3,2,1,0:T(8,128)(2,1)} async-done(((bf16[32,1,96,1024]{3,2,1,0:T(8,128)(2,1)}), bf16[32,1,96,1024]{3,2,1,0:T(8,128)(2,1)}, u32[]{:S(2)}, u32[]{:S(2)}) %all-to-all-start.3) | async-done | bytes 6291488 | tf_op jit(solution)/shard_map/all_to_all | solution.py:201
  311.2 14.5 %gather_fusion.1 = bf16[2048,1024]{1,0:T(8,128)(2,1)} fusion(bf16[3072,1024]{1,0:T(8,128)(2,1)} %bitcast.69, s32[2048]{0:T(1024)S(1)} %broadcast_clamp_fusion), kind=kCustom, calls=%fused_computation.1 | custom fusion | bytes 8396800 | tf_op jit(solution)/shard_map/gather | solution.py:204
  333.8 18.7 %gather_fusion.2 = bf16[3072,1024]{1,0:T(8,128)(2,1)} fusion(bf16[2049,1024]{1,0:T(8,128)(2,1)} %concatenate.32, s32[3072]{0:T(1024)S(1)} %get-tuple-element.306), kind=kCustom, calls=%fused_computation.2 | custom fusion | bytes 12595200 | tf_op jit(solution)/shard_map/gather | solution.py:223
  352.5 79.8 %all_to_all.40 = bf16[32,1,96,1024]{3,2,1,0:T(8,128)(2,1)S(1)} all-to-all(bf16[32,1,96,1024]{3,2,1,0:T(8,128)(2,1)} %bitcast.472), channel_id=1, replica_groups=mesh['dp'=32,'tensor'=4] {'dp'}, dimensions={0} | all-to-all | bytes 12582912 | tf_op jit(solution)/shard_map/all_to_all | solution.py:224
  432.3 12.8 %fusion.97 = (bf16[32,96,512]{2,1,0:T(8,128)(2,1)}, bf16[32,1,96,512]{3,2,0,1:T(8,128)(2,1)}) fusion(f32[512,32,96]{0,2,1:T(8,128)} %copy-done.22, f32[512,32,96]{0,2,1:T(8,128)} %copy-done.21, bf16[32,1,96,1024]{3,2,1,0:T(8,128)(2,1)S(1)} %all_to_all.40, bf16[512,3072]{0,1:T(8,128)(2,1)} %all-gather.2.cloned.1.call-done), kind=kOutput, calls=%fused_computation.113 | convolution fusion | flops 3241672704 | bytes 26214400 | tf_op jit(solution)/shard_map/secd,efd->secf/dot_general | solution.py:225
  451.1 8.5 fusion.70
  459.6 7.3 all-to-all-start.5
  467.2 8.2 fusion.117
  475.4 65.2 %all-to-all-done.5 = bf16[32,1,96,1024]{3,2,1,0:T(8,128)(2,1)} async-done(((bf16[32,1,96,1024]{3,2,1,0:T(8,128)(2,1)}), bf16[32,1,96,1024]{3,2,1,0:T(8,128)(2,1)}, u32[]{:S(2)}, u32[]{:S(2)}) %all-to-all-start.5) | async-done | bytes 6291488 | tf_op jit(solution)/shard_map/all_to_all | solution.py:252
  540.6 14.5 %gather_fusion.3 = bf16[2048,1024]{1,0:T(8,128)(2,1)} fusion(bf16[3072,1024]{1,0:T(8,128)(2,1)} %bitcast.94, s32[2048]{0:T(1024)S(1)} %broadcast_clamp_fusion), kind=kCustom, calls=%fused_computation.3 | custom fusion | bytes 8396800 | tf_op jit(solution)/shard_map/gather | solution.py:255
  570.2 7.3 fusion.109
  577.6 6.3 fusion.114
  597.1 130.5 %while.31 = (s32[]{:T(128)}, f32[2,512,2,2,64]{1,0,4,3,2:T(2,128)}, f32[2,1024,2,64]{1,3,2,0:T(8,128)}, f32[2,1024,2,64]{1,3,2,0:T(8,128)}, s32[2]{0:T(128)S(1)}...) while((s32[]{:T(128)}, f32[2,512,2,2,64]{1,0,4,3,2:T(2,128)}, ...), condition=%wide.region_21.22_spmd, body=%wide.region_19.21_spmd.sunk | while | flops 1397234176 | bytes 87873016 | solution.py:291
  610.3 17.3 %fusion.235 = f32[1,512,2,2,64]{1,4,3,2,0:T(8,128)S(1)} fusion(f32[2,512,2,1024]{3,1,2,0:T(8,128)} %fusion.233, f32[2,512,2,1024]{3,1,2,0:T(8,128)} %fusion.234, f32[2,2,512]{2,1,0:T(2,128)S(1)} %dynamic-slice_bitcast_fusion.2, pred[512,1024]{1,0:T(8,128)(4,1)S(1)} %iota_compare_fusion.8, bf16[1024,2,64]{0,2,1:T(8,128)(2,1)S(1)} %get-tuple-element.502), kind=kOutput, calls=%fused_computation.46.clone.1 | convolution fusion | flops 291507200 | bytes 18096128 | tf_op jit(solution)/shard_map/while/body/eval_jaxpr/hgqk,khd->qhgd/dot_general | solution.py:280
  628.2 10.4 %dynamic_update_slice.47 = f32[2,512,2,2,64]{1,0,4,3,2:T(2,128)} dynamic-update-slice(f32[2,512,2,2,64]{1,0,4,3,2:T(2,128)} %get-tuple-element.481, f32[1,512,2,2,64]{1,0,4,3,2:T(1,128)S(1)} %copy.125, s32[]{:T(128)} %get-tuple-element.480, s32[]{:T(128)} %constant.204.clone.1..sunk.1, s32[]{:T(128)} %constant.204.clone.1..sunk.1, s32[]{:T(128)} %constant.204.clone.1..sunk.1, ...) | dynamic-update-slice | bytes 1048580 | tf_op jit(solution)/shard_map/while/body/jit(dynamic_update_index_in_dim)/dynamic_update_slice | solution.py:291
  638.6 18.5 %fusion.236 = f32[2,1024,2,64]{1,3,2,0:T(8,128)} fusion(f32[2,1024,2,64]{1,3,2,0:T(8,128)} %get-tuple-element.482, s32[]{:T(128)} %get-tuple-element.480, f32[2,512,2,1024]{3,1,2,0:T(8,128)} %fusion.233, f32[2,512,2,1024]{3,1,2,0:T(8,128)} %fusion.234, f32[2,2,512]{2,1,0:T(2,128)S(1)} %dynamic-slice_bitcast_fusion.2, ...), kind=kOutput, calls=%fused_computation.48.clone.1 | convolution fusion | flops 291507200 | bytes 35406340 | tf_op jit(solution)/shard_map/while/body/eval_jaxpr/hgqk,qhgd->khd/dot_general | solution.py:283
  675.3 17.2 %fusion.235 = f32[1,512,2,2,64]{1,4,3,2,0:T(8,128)S(1)} fusion(f32[2,512,2,1024]{3,1,2,0:T(8,128)} %fusion.233, f32[2,512,2,1024]{3,1,2,0:T(8,128)} %fusion.234, f32[2,2,512]{2,1,0:T(2,128)S(1)} %dynamic-slice_bitcast_fusion.2, pred[512,1024]{1,0:T(8,128)(4,1)S(1)} %iota_compare_fusion.8, bf16[1024,2,64]{0,2,1:T(8,128)(2,1)S(1)} %get-tuple-element.502), kind=kOutput, calls=%fused_computation.46.clone.1 | convolution fusion | flops 291507200 | bytes 18096128 | tf_op jit(solution)/shard_map/while/body/eval_jaxpr/hgqk,khd->qhgd/dot_general | solution.py:280
  693.0 10.4 %dynamic_update_slice.47 = f32[2,512,2,2,64]{1,0,4,3,2:T(2,128)} dynamic-update-slice(f32[2,512,2,2,64]{1,0,4,3,2:T(2,128)} %get-tuple-element.481, f32[1,512,2,2,64]{1,0,4,3,2:T(1,128)S(1)} %copy.125, s32[]{:T(128)} %get-tuple-element.480, s32[]{:T(128)} %constant.204.clone.1..sunk.1, s32[]{:T(128)} %constant.204.clone.1..sunk.1, s32[]{:T(128)} %constant.204.clone.1..sunk.1, ...) | dynamic-update-slice | bytes 1048580 | tf_op jit(solution)/shard_map/while/body/jit(dynamic_update_index_in_dim)/dynamic_update_slice | solution.py:291
  703.4 18.5 %fusion.236 = f32[2,1024,2,64]{1,3,2,0:T(8,128)} fusion(f32[2,1024,2,64]{1,3,2,0:T(8,128)} %get-tuple-element.482, s32[]{:T(128)} %get-tuple-element.480, f32[2,512,2,1024]{3,1,2,0:T(8,128)} %fusion.233, f32[2,512,2,1024]{3,1,2,0:T(8,128)} %fusion.234, f32[2,2,512]{2,1,0:T(2,128)S(1)} %dynamic-slice_bitcast_fusion.2, ...), kind=kOutput, calls=%fused_computation.48.clone.1 | convolution fusion | flops 291507200 | bytes 35406340 | tf_op jit(solution)/shard_map/while/body/eval_jaxpr/hgqk,qhgd->khd/dot_general | solution.py:283
  765.6 94.9 %all-reduce.13.cloned.1.call-done = (bf16[1024,256]{1,0:T(8,128)(2,1)}, bf16[1024,128]{1,0:T(8,128)(2,1)}, bf16[1024,128]{1,0:T(8,128)(2,1)}, bf16[256,1024]{1,0:T(8,128)(2,1)}) async-done(((bf16[1024,256]{1,0:T(8,128)(2,1)}, bf16[1024,128]{1,0:T(8,128)(2,1)}, bf16[1024,128]{1,0:T(8,128)(2,1)}, bf16[256,1024]{1,0:T(8,128)(2,1)}), (bf16[1024,256]{1,0:T(8,128)(2,1)}, bf16[1024,128]{1,0:T(8,128)(2,1)}, ...) | async-done | bytes 1572880 | tf_op jit(solution)/shard_map/psum | solution.py:323
  874.0 63.4 %all-reduce.6 = (f32[1024]{0:T(1024)}, f32[1024]{0:T(1024)}) all-reduce(f32[1024]{0:T(1024)S(1)} %get-tuple-element.242, f32[1024]{0:T(1024)S(1)} %get-tuple-element.240), channel_id=1, replica_groups=mesh['dp'=32,'tensor'=4] {'dp','tensor'}, use_global_device_ids=true, to_apply=%region_27.28 | all-reduce | flops 2048 | bytes 16384 | tf_op jit(solution)/shard_map/psum | solution.py:328
  937.3 66.6 %all-reduce.11.cloned.1.call-done = f32[1024,32]{0,1:T(8,128)} async-done(((f32[1024,32]{0,1:T(8,128)}), f32[1024,32]{0,1:T(8,128)}) %all-reduce.11.cloned.1.call-update) | async-done | bytes 131088 | tf_op jit(solution)/shard_map/psum | solution.py:328
  (284 shorter events, 201.4 us)
Async XLA Ops:
  7.2 66.4 %copy-start = (bf16[256,1024]{1,0:T(8,128)(2,1)S(1)}, bf16[256,1024]{1,0:T(8,128)(2,1)}, u32[]{:S(2)}) copy-start(bf16[256,1024]{1,0:T(8,128)(2,1)} %param.24) | copy-start | bytes 1572868
  12.5 29.8 %all-to-all-start = ((bf16[4,256,1024]{2,1,0:T(8,128)(2,1)}), bf16[4,256,1024]{2,1,0:T(8,128)(2,1)S(1)}, u32[]{:S(2)}, u32[]{:S(2)}) async-start(bf16[4,256,1024]{2,1,0:T(8,128)(2,1)} %broadcast_in_dim.158), calls=%async_computation | async-start | bytes 4194304 | tf_op jit(solution)/shard_map/all_to_all | solution.py:17
  19.9 26.5 %copy-start.15 = (f32[1024,64]{0,1:T(8,128)}, f32[1024,64]{0,1:T(8,128)S(1)}, u32[]{:S(2)}) copy-start(f32[1024,64]{0,1:T(8,128)S(1)} %get-tuple-element.312) | copy-start | bytes 786436
  19.9 26.5 %copy-start.17 = (f32[1024,64]{0,1:T(8,128)}, f32[1024,64]{0,1:T(8,128)S(1)}, u32[]{:S(2)}) copy-start(f32[1024,64]{0,1:T(8,128)S(1)} %get-tuple-element.311) | copy-start | bytes 786436
  71.7 20.7 %copy-start.7 = (bf16[1024,2,64]{0,2,1:T(8,128)(2,1)}, bf16[1024,2,64]{0,2,1:T(8,128)(2,1)S(1)}, u32[]{:S(2)}) copy-start(bf16[1024,2,64]{0,2,1:T(8,128)(2,1)S(1)} %get-tuple-element.539) | copy-start | bytes 786436
  71.7 20.7 %copy-start.9 = (bf16[1024,2,64]{0,2,1:T(8,128)(2,1)}, bf16[1024,2,64]{0,2,1:T(8,128)(2,1)S(1)}, u32[]{:S(2)}) copy-start(bf16[1024,2,64]{0,2,1:T(8,128)(2,1)S(1)} %get-tuple-element.540) | copy-start | bytes 786436
  71.7 20.7 %copy-start.45 = (f32[2,2,2,512,1]{3,2,1,4,0:T(2,128)}, f32[2,2,2,512,1]{3,2,1,4,0:T(2,128)S(1)}, u32[]{:S(2)}) copy-start(f32[2,2,2,512,1]{3,2,1,4,0:T(2,128)S(1)} %get-tuple-element.471) | copy-start | bytes 49156
  73.6 34.3 %copy-start.5 = (bf16[256,1024]{1,0:T(8,128)(2,1)S(1)}, bf16[256,1024]{1,0:T(8,128)(2,1)}, u32[]{:S(2)}) copy-start(bf16[256,1024]{1,0:T(8,128)(2,1)} %param.18) | copy-start | bytes 1572868
  75.7 32.5 %copy-start.48 = (f32[1024]{0:T(1024)S(1)}, f32[1024]{0:T(1024)}, u32[]{:S(2)}) copy-start(f32[1024]{0:T(1024)} %param.25) | copy-start | bytes 12292
  75.7 30.1 %all-to-all-start.1 = ((bf16[4,256,1024]{2,1,0:T(8,128)(2,1)}), bf16[4,256,1024]{2,1,0:T(8,128)(2,1)}, u32[]{:S(2)}, u32[]{:S(2)}) async-start(bf16[4,256,1024]{2,1,0:T(8,128)(2,1)} %bitcast.475), calls=%async_computation.1 | async-start | bytes 4194304 | tf_op jit(solution)/shard_map/all_to_all | solution.py:38
  108.1 453.1 %copy-start.3 = (f32[256,1024]{1,0:T(8,128)}, f32[256,1024]{1,0:T(8,128)S(1)}, u32[]{:S(2)}) copy-start(f32[256,1024]{1,0:T(8,128)S(1)} %get-tuple-element.289) | copy-start | bytes 3145732
  108.3 130.2 %copy-start.13 = (bf16[256,1024]{1,0:T(8,128)(2,1)}, bf16[256,1024]{1,0:T(8,128)(2,1)S(1)}, u32[]{:S(2)}) copy-start(bf16[256,1024]{1,0:T(8,128)(2,1)S(1)} %multiply_convert_fusion) | copy-start | bytes 1572868
  122.4 82.3 %all-to-all-start.2 = ((bf16[32,1,96,1024]{3,2,1,0:T(8,128)(2,1)}), bf16[32,1,96,1024]{3,2,1,0:T(8,128)(2,1)}, u32[]{:S(2)}, u32[]{:S(2)}) async-start(bf16[32,1,96,1024]{3,2,1,0:T(8,128)(2,1)} %bitcast.471), calls=%async_computation.2 | async-start | bytes 12582912 | tf_op jit(solution)/shard_map/all_to_all | solution.py:194
  131.0 45.8 %all-gather.2.cloned.1.call-start = ((), (), s32[]{:S(2)}) async-start(), calls=%async_computation.10 | async-start | bytes 3932160 | tf_op jit(solution)/shard_map/all_gather | solution.py:46
  228.3 82.8 %all-to-all-start.3 = ((bf16[32,1,96,1024]{3,2,1,0:T(8,128)(2,1)}), bf16[32,1,96,1024]{3,2,1,0:T(8,128)(2,1)}, u32[]{:S(2)}, u32[]{:S(2)}) async-start(bf16[32,1,96,1024]{3,2,1,0:T(8,128)(2,1)} %convert_bitcast_fusion), calls=%async_computation.3 | async-start | bytes 12582912 | tf_op jit(solution)/shard_map/all_to_all | solution.py:201
  330.5 136.7 %copy-start.43 = (f32[256,8]{0,1:T(8,128)}, f32[256,8]{0,1:T(8,128)S(1)}, u32[]{:S(2)}) copy-start(f32[256,8]{0,1:T(8,128)S(1)} %get-tuple-element.287) | copy-start | bytes 24580
  459.6 81.1 %all-to-all-start.5 = ((bf16[32,1,96,1024]{3,2,1,0:T(8,128)(2,1)}), bf16[32,1,96,1024]{3,2,1,0:T(8,128)(2,1)}, u32[]{:S(2)}, u32[]{:S(2)}) async-start(bf16[32,1,96,1024]{3,2,1,0:T(8,128)(2,1)} %fusion.70), calls=%async_computation.5 | async-start | bytes 12582912 | tf_op jit(solution)/shard_map/all_to_all | solution.py:252
  466.9 289.4 %reduce-scatter.5.cloned.1.call-start = ((), (), s32[]{:S(2)}) async-start(), calls=%async_computation.12 | async-start | bytes 1310720 | tf_op jit(solution)/shard_map/reduce_scatter | solution.py:248
  564.1 30.6 %all-to-all-start.6 = ((bf16[4,256,1024]{2,1,0:T(8,128)(2,1)}), bf16[4,256,1024]{2,1,0:T(8,128)(2,1)}, u32[]{:S(2)}, u32[]{:S(2)}) async-start(bf16[4,256,1024]{2,1,0:T(8,128)(2,1)} %broadcast_in_dim.170), calls=%async_computation.6 | async-start | bytes 4194304 | tf_op jit(solution)/shard_map/all_to_all | solution.py:17
  570.0 188.0 %reduce-scatter.7.cloned.1.call-start = ((), (), s32[]{:S(2)}) async-start(), calls=%async_computation.13 | async-start | bytes 2621440
  597.1 135.4 %copy-start.16 = (f32[1024,64]{0,1:T(8,128)S(1)}, f32[1024,64]{0,1:T(8,128)}, u32[]{:S(2)}) copy-start(f32[1024,64]{0,1:T(8,128)} %copy-done.15) | copy-start | bytes 786436
  638.6 18.5 %copy-start.26 = (bf16[1024,2,2,64]{0,3,2,1:T(8,128)(2,1)S(1)}, bf16[1024,2,2,64]{0,3,2,1:T(8,128)(2,1)}, u32[]{:S(2)}) copy-start(bf16[1024,2,2,64]{0,3,2,1:T(8,128)(2,1)} %copy-done.25) | copy-start | bytes 1572868 | tf_op jit(solution)/shard_map/while
  703.4 18.5 %copy-start.26 = (bf16[1024,2,2,64]{0,3,2,1:T(8,128)(2,1)S(1)}, bf16[1024,2,2,64]{0,3,2,1:T(8,128)(2,1)}, u32[]{:S(2)}) copy-start(bf16[1024,2,2,64]{0,3,2,1:T(8,128)(2,1)} %copy-done.25) | copy-start | bytes 1572868 | tf_op jit(solution)/shard_map/while
  737.1 131.2 %all-to-all-start.7 = ((bf16[4,256,1024]{2,1,0:T(8,128)(2,1)}), bf16[4,256,1024]{2,1,0:T(8,128)(2,1)}, u32[]{:S(2)}, u32[]{:S(2)}) async-start(bf16[4,256,1024]{2,1,0:T(8,128)(2,1)} %bitcast.477), calls=%async_computation.7 | async-start | bytes 4194304 | tf_op jit(solution)/shard_map/all_to_all | solution.py:38
  742.9 117.6 %all-reduce.13.cloned.1.call-start = ((), (), s32[]{:S(2)}) async-start(), calls=%async_computation.14 | async-start | bytes 3145728 | tf_op jit(solution)/shard_map/psum | solution.py:323
  750.7 253.2 %all-reduce.11.cloned.1.call-start = ((), (), s32[]{:S(2)}) async-start(), calls=%async_computation.11 | async-start | bytes 262144 | tf_op jit(solution)/shard_map/psum | solution.py:328
  759.5 110.9 %copy-start.6 = (bf16[256,1024]{1,0:T(8,128)(2,1)S(1)}, bf16[256,1024]{1,0:T(8,128)(2,1)}, u32[]{:S(2)}) copy-start(bf16[256,1024]{1,0:T(8,128)(2,1)} %param.18) | copy-start | bytes 1572868
  759.5 110.9 %copy-start.49 = (f32[1024]{0:T(1024)S(1)}, f32[1024]{0:T(1024)}, u32[]{:S(2)}) copy-start(f32[1024]{0:T(1024)} %param.20) | copy-start | bytes 12292
  759.5 110.9 %copy-start.51 = (f32[256]{0:T(256)S(1)}, f32[256]{0:T(256)}, u32[]{:S(2)}) copy-start(f32[256]{0:T(256)} %copy-done.50) | copy-start | bytes 3076
  761.2 109.6 %copy-start.53 = (f32[256]{0:T(256)S(1)}, f32[256]{0:T(256)}, u32[]{:S(2)}) copy-start(f32[256]{0:T(256)} %copy-done.52) | copy-start | bytes 3076
  761.2 109.6 %copy-start.4 = (f32[256,1024]{1,0:T(8,128)S(1)}, f32[256,1024]{1,0:T(8,128)}, u32[]{:S(2)}) copy-start(f32[256,1024]{1,0:T(8,128)} %copy-done.3) | copy-start | bytes 3145732
  761.2 109.6 %copy-start.12 = (f32[256,1024]{1,0:T(8,128)S(1)}, f32[256,1024]{1,0:T(8,128)}, u32[]{:S(2)}) copy-start(f32[256,1024]{1,0:T(8,128)} %copy-done.11) | copy-start | bytes 3145732
  (41 other events, 246.6 us)
Sparse Core Ops, SparseCore 0:
  134.1 42.6 all-gather.1
  475.5 21.4 reduce-scatter.4
  591.8 29.1 reduce-scatter.6
  750.9 109.5 all-reduce.12
  866.4 137.5 all-reduce.10
where the time goes:
time: 1030 us; the launch traced here: 1010 us
  waiting for transfers between devices  402 us (39%)
  matrix products  210 us (20%)
  blocking collectives  143 us (14%)
  local copies, waits for them, and re-layouts  129 us (13%)
  other arithmetic  54.1 us (5%)
  starting transfers between devices  48.2 us (5%)
  between operations  15 us (1%)
  loops' own time  11.3 us (1%)
    psum x1, waiting for transfers between devices, shards(): lax.psum(query_grad.astype(jnp.bfloat16), 'dp').astype(jnp.float32)  94.9 us
    all_to_all x1, blocking collectives, shards(): lax.all_to_all(send_grads, 'dp', split_axis=0, concat_axis=0, tiled=True)  79.8 us
    all_to_all x1, waiting for transfers between devices, shards(): lax.all_to_all(out_rows_low, 'dp', split_axis=0, concat_axis=0, tiled=True)  72.3 us
    psum x1, waiting for transfers between devices, shards(): lax.psum((gain_attn_part, gain_moe_part, router_part), ('dp', 'tensor'))  66.6 us
    all_to_all x1, waiting for transfers between devices, shards(): lax.all_to_all(d_in_full.astype(jnp.bfloat16), 'dp', split_axis=0, concat...  65.2 us
    psum x1, blocking collectives, shards(): lax.psum((gain_attn_part, gain_moe_part, router_part), ('dp', 'tensor'))  63.4 us
    all_gather x1, waiting for transfers between devices, gather_turned(): result = lax.all_gather(both, axis, axis=0, tiled=True)  44.6 us
    dot_general x2, matrix products, backward_block(): jnp.einsum('hgqk,qhgd->khd', d_raw, query_block, preferred_element_type=j...  37.1 us
  transfers between devices with their start and end apart: 12, of which 9 were waited for; matrix products, arithmetic and copies ran while one was open for 24% of the time, Pallas kernels for 0%

commit v1 on v0

v1 whole, which is shorter than its diff:
```python
import functools
import math

import jax
import jax.numpy as jnp
from jax import lax
from jax.experimental import pallas as pl
from jax.experimental.pallas import tpu as pltpu
from jax.sharding import PartitionSpec as P

BF = jnp.bfloat16
F32 = jnp.float32
NORM_EPS = 1e-05
HEAD = 64
SEQ = 1024
ROWS = 256
WIDTH = 1024
HALF = 512
FF = 512
SLOTS = 32
CAP = 96
VMEM = 58 * 1024 * 1024

NN = (((1,), (0,)), ((), ()))
NT = (((1,), (1,)), ((), ()))
TN = (((0,), (0,)), ((), ()))


def mm(a, b, dims=NN):
    return lax.dot_general(a, b, dims, preferred_element_type=F32)


def _dp_pairs(dz, dx, dc):
    pairs = []
    for z in range(4):
        for x in range(4):
            for c in range(2):
                src = ((z + dz) % 4) * 8 + ((x + dx) % 4) * 2 + (c + dc) % 2
                pairs.append((src, z * 8 + x * 2 + c))
    return pairs


def from_z(v, d):
    return lax.ppermute(v, "dp", _dp_pairs(d, 0, 0))


def from_x(v, d):
    return lax.ppermute(v, "dp", _dp_pairs(0, d, 0))


def from_core(v):
    return lax.ppermute(v, "dp", _dp_pairs(0, 0, 1))


def from_y(v, d):
    return lax.ppermute(v, "tensor", [((i + d) % 4, i) for i in range(4)])


def low(v):
    return v.astype(BF)


def wide(v):
    return v.astype(F32)


def ring_gather(own, get):
    half = own.shape[0] // 2
    plus, minus = get(own, 1), get(own, -1)
    far = jnp.concatenate([get(plus[:half], 1), get(minus[half:], -1)], axis=0)
    return plus, far, minus


def ring_sum(blocks, get):
    own, plus, far, minus = blocks
    half = own.shape[0] // 2
    far_low, far_high = get(far[:half], -1), get(far[half:], 1)
    to_plus = jnp.concatenate([low(wide(plus[:half]) + wide(far_low)), plus[half:]], axis=0)
    to_minus = jnp.concatenate([minus[:half], low(wide(minus[half:]) + wide(far_high))], axis=0)
    return wide(own) + wide(get(to_plus, -1)) + wide(get(to_minus, 1))


def gather_direct(own, get):
    half = own.shape[0] // 2
    return get(own, 1), get(own[:half], 2), get(own[half:], -2), get(own, -1)


def sum_direct(own, plus, far_low, far_high, minus, get):
    far = jnp.concatenate([get(far_low, 2), get(far_high, -2)], axis=0)
    return wide(own) + wide(get(plus, -1)) + wide(get(minus, 1)) + wide(far)


def plane_gather(rows):
    a, b = rows[None, :, :HALF], rows[None, :, HALF:]

    def ring4(v, get):
        plus, minus = get(v, 1), get(v, -1)
        cut = ROWS // 2
        far = jnp.concatenate([get(plus[:, :cut], 1), get(minus[:, cut:], -1)], axis=1)
        return jnp.concatenate([v, plus, far, minus], axis=0)

    a4, b4 = ring4(a, from_z), ring4(b, from_x)
    return (a4, *ring_gather(a4, from_x)), (b4, *ring_gather(b4, from_z))


def plane_sum(a_blocks, b_blocks):
    sa = low(ring_sum(a_blocks, from_x))
    sb = low(ring_sum(b_blocks, from_z))
    ra = ring_sum([sa[i] for i in range(4)], from_z)
    rb = ring_sum([sb[i] for i in range(4)], from_x)
    return jnp.concatenate([ra, rb], axis=1)


def ring_position(dp):
    return dp // 8, (dp // 2) % 4, dp % 2


def dp_sum(v, dp):
    _, x, c = ring_position(dp)
    half = v.shape[0] // 2
    part = half // 4
    keep = lax.dynamic_slice_in_dim(v, c * half, half, 0)
    send = lax.dynamic_slice_in_dim(v, (1 - c) * half, half, 0)
    s = low(wide(keep) + wide(from_core(send)))
    b = [lax.dynamic_slice_in_dim(s, ((x + r) % 4) * part, part, 0) for r in range(4)]
    s = low(sum_direct(b[0], b[1], b[2][: part // 2], b[2][part // 2 :], b[3], from_x))
    p, fl, fh, m = gather_direct(s, from_z)
    s = low(wide(s) + wide(p) + wide(m) + jnp.concatenate([wide(fl), wide(fh)], axis=0))
    p, fl, fh, m = gather_direct(s, from_x)
    whole = jnp.concatenate([s, p, fl, fh, m], axis=0)
    whole = jnp.concatenate([whole, whole], axis=0)
    whole = lax.dynamic_slice_in_dim(whole, ((4 - x) % 4) * part, half, 0)
    other = from_core(whole)
    return jnp.where(
        c == 0,
        jnp.concatenate([whole, other], axis=0),
        jnp.concatenate([other, whole], axis=0),
    )


def tensor_sum(v):
    return v + from_y(v, 1) + from_y(v, 2) + from_y(v, 3)


def _block_starts(y):
    starts = []
    for r in range(4):
        off = lax.rem(y + r, 4) * ROWS
        if r == 2:
            starts += [off, off + ROWS // 2]
        else:
            starts.append(off)
    return [pl.multiple_of(s, 128) for s in starts]


def attention_forward_kernel(
    y_ref, n0, n1, n2, n3, n4, w_ref, wo_ref, cos_ref, sin_ref,
    qkv_ref, o_ref, lse_ref, p0, p1, p2, p3, p4,
):
    starts = _block_starts(y_ref[0])
    for start, ref in zip(starts, (n0, n1, n2, n3, n4)):
        width = ref.shape[0]
        at = pl.ds(start, width)
        t = mm(w_ref[...], ref[...], NT)
        cos, sin = cos_ref[:, at], sin_ref[:, at]
        for h in range(6):
            a, b = t[64 * h : 64 * h + 32], t[64 * h + 32 : 64 * h + 64]
            ra, rb = a * cos - b * sin, b * cos + a * sin
            if h < 4:
                ra, rb = ra * 0.125, rb * 0.125
            qkv_ref[64 * h : 64 * h + 32, at] = low(ra)
            qkv_ref[64 * h + 32 : 64 * h + 64, at] = low(rb)
        qkv_ref[384:512, at] = low(t[384:])
    key_at = lax.broadcasted_iota(jnp.int32, (ROWS, 2 * ROWS), 0)
    query_at = lax.broadcasted_iota(jnp.int32, (ROWS, 2 * ROWS), 1)
    allowed = key_at <= jnp.bitwise_and(query_at, ROWS - 1)
    for g in range(2):
        keys = qkv_ref[256 + 64 * g : 320 + 64 * g, :].T
        values = qkv_ref[384 + 64 * g : 448 + 64 * g, :]
        for i in range(4):
            here = slice(i * ROWS, (i + 1) * ROWS)
            q2 = jnp.concatenate(
                [qkv_ref[128 * g : 128 * g + 64, here], qkv_ref[128 * g + 64 : 128 * g + 128, here]],
                axis=1,
            )
            tiles = []
            for j in range(i + 1):
                s = mm(keys[j * ROWS : (j + 1) * ROWS], q2)
                if j == i:
                    s = jnp.where(allowed, s, -jnp.inf)
                tiles.append(s)
            peak = tiles[0].max(axis=0, keepdims=True)
            for s in tiles[1:]:
                peak = jnp.maximum(peak, s.max(axis=0, keepdims=True))
            total = jnp.zeros_like(peak)
            mixed = jnp.zeros((HEAD, 2 * ROWS), F32)
            for j, s in enumerate(tiles):
                e = jnp.exp(s - peak)
                total = total + e.sum(axis=0, keepdims=True)
                mixed = mixed + mm(values[:, j * ROWS : (j + 1) * ROWS], low(e))
            mixed = mixed / total
            lse = peak + jnp.log(total)
            o_ref[128 * g : 128 * g + 64, here] = mixed[:, :ROWS]
            o_ref[128 * g + 64 : 128 * g + 128, here] = mixed[:, ROWS:]
            lse_ref[2 * g : 2 * g + 1, here] = lse[:, :ROWS]
            lse_ref[2 * g + 1 : 2 * g + 2, here] = lse[:, ROWS:]
    lse_ref[4:8, :] = jnp.zeros((4, SEQ), F32)
    for start, ref in zip(starts, (p0, p1, p2, p3, p4)):
        att = low(o_ref[:, pl.ds(start, ref.shape[0])])
        ref[...] = low(mm(att.T, wo_ref[...]))


PIECES = (ROWS, ROWS, ROWS // 2, ROWS // 2, ROWS)


def attention_forward(y, blocks, w_t, w_out, cos, sin):
    smem = pl.BlockSpec(memory_space=pltpu.SMEM)
    vmem = pl.BlockSpec(memory_space=pltpu.VMEM)
    return pl.pallas_call(
        attention_forward_kernel,
        out_shape=(
            jax.ShapeDtypeStruct((512, SEQ), BF),
            jax.ShapeDtypeStruct((256, SEQ), F32),
            jax.ShapeDtypeStruct((8, SEQ), F32),
            *[jax.ShapeDtypeStruct((w, WIDTH), BF) for w in PIECES],
        ),
        in_specs=[smem] + [vmem] * 9,
        out_specs=[vmem] * 8,
        compiler_params=pltpu.CompilerParams(vmem_limit_bytes=VMEM),
        cost_estimate=pl.CostEstimate(flops=8_000_000_000, bytes_accessed=10_000_000, transcendentals=3_000_000),
        name="attention_forward",
    )(y, *blocks, w_t, w_out, cos, sin)


def out_gradient_kernel(y_ref, d0, d1, d2, d3, d4, o_ref, g_ref):
    total = jnp.zeros((256, WIDTH), F32)
    for start, ref in zip(_block_starts(y_ref[0]), (d0, d1, d2, d3, d4)):
        total = total + mm(low(o_ref[:, pl.ds(start, ref.shape[0])]), ref[...])
    g_ref[...] = low(total)


def out_gradient(y, blocks, o):
    smem = pl.BlockSpec(memory_space=pltpu.SMEM)
    vmem = pl.BlockSpec(memory_space=pltpu.VMEM)
    return pl.pallas_call(
        out_gradient_kernel,
        out_shape=jax.ShapeDtypeStruct((256, WIDTH), BF),
        in_specs=[smem] + [vmem] * 6,
        out_specs=vmem,
        compiler_params=pltpu.CompilerParams(vmem_limit_bytes=VMEM),
        cost_estimate=pl.CostEstimate(flops=540_000_000, bytes_accessed=4_000_000, transcendentals=0),
        name="out_gradient",
    )(y, *blocks, o)


def attention_backward_kernel(
    g, y_ref, d0, d1, d2, d3, d4, x0, x1, x2, x3, x4, qkv_ref, o_ref, lse_ref, wo_ref, cos_ref, sin_ref,
    dqkv_ref, gw_ref, do_ref, delta_ref, dk_ref, dv_ref,
):
    starts = _block_starts(y_ref[0])
    heads = slice(128 * g, 128 * g + 128)
    for start, ref in zip(starts, (d0, d1, d2, d3, d4)):
        do_ref[:, pl.ds(start, ref.shape[0])] = low(mm(wo_ref[heads, :], ref[...], NT))
    prod = o_ref[heads, :] * wide(do_ref[...])
    delta_ref[0:1, :] = prod[:64].sum(axis=0, keepdims=True)
    delta_ref[1:2, :] = prod[64:].sum(axis=0, keepdims=True)
    keys_t = qkv_ref[256 + 64 * g : 320 + 64 * g, :]
    keys = keys_t.T
    values = qkv_ref[384 + 64 * g : 448 + 64 * g, :].T
    dk_ref[...] = jnp.zeros_like(dk_ref)
    dv_ref[...] = jnp.zeros_like(dv_ref)
    key_at = lax.broadcasted_iota(jnp.int32, (ROWS, 2 * ROWS), 0)
    query_at = lax.broadcasted_iota(jnp.int32, (ROWS, 2 * ROWS), 1)
    allowed = key_at <= jnp.bitwise_and(query_at, ROWS - 1)
    for i in range(4):
        here = slice(i * ROWS, (i + 1) * ROWS)

        def pair(ref, base, step):
            return jnp.concatenate(
                [ref[base : base + step, here], ref[base + step : base + 2 * step, here]], axis=1
            )

        q2 = pair(qkv_ref, 128 * g, 64)
        do2 = pair(do_ref, 0, 64)
        lse2 = pair(lse_ref, 2 * g, 1)
        delta2 = pair(delta_ref, 0, 1)
        dq = jnp.zeros((HEAD, 2 * ROWS), F32)
        for j in range(i + 1):
            at = slice(j * ROWS, (j + 1) * ROWS)
            s = mm(keys[at], q2)
            p = jnp.exp(s - lse2)
            if j == i:
                p = jnp.where(allowed, p, 0.0)
            dp = mm(values[at], do2)
            ds = low(p * (dp - delta2))
            dq = dq + mm(keys_t[:, at], ds)
            dk_ref[:, at] += mm(q2, ds, NT)
            dv_ref[:, at] += mm(do2, low(p), NT)
        cos, sin = cos_ref[:, here], sin_ref[:, here]
        dq = dq * 0.125
        for h in range(2):
            a, b = dq[:32, h * ROWS : (h + 1) * ROWS], dq[32:, h * ROWS : (h + 1) * ROWS]
            dqkv_ref[64 * h : 64 * h + 32, here] = low(a * cos + b * sin)
            dqkv_ref[64 * h + 32 : 64 * h + 64, here] = low(b * cos - a * sin)
    a, b = dk_ref[:32, :], dk_ref[32:, :]
    dqkv_ref[128:160, :] = low(a * cos_ref[...] + b * sin_ref[...])
    dqkv_ref[160:192, :] = low(b * cos_ref[...] - a * sin_ref[...])
    dqkv_ref[192:256, :] = low(dv_ref[...])
    total = jnp.zeros((256, WIDTH), F32)
    for start, ref in zip(starts, (x0, x1, x2, x3, x4)):
        total = total + mm(dqkv_ref[:, pl.ds(start, ref.shape[0])], ref[...])
    gw_ref[...] = low(total)


def attention_backward(g, y, d_blocks, x_blocks, qkv, o, lse, w_out, cos, sin):
    smem = pl.BlockSpec(memory_space=pltpu.SMEM)
    vmem = pl.BlockSpec(memory_space=pltpu.VMEM)
    return pl.pallas_call(
        functools.partial(attention_backward_kernel, g),
        out_shape=(
            jax.ShapeDtypeStruct((256, SEQ), BF),
            jax.ShapeDtypeStruct((256, WIDTH), BF),
        ),
        in_specs=[smem] + [vmem] * 16,
        out_specs=[vmem] * 2,
        scratch_shapes=[
            pltpu.VMEM((128, SEQ), BF),
            pltpu.VMEM((8, SEQ), F32),
            pltpu.VMEM((64, SEQ), F32),
            pltpu.VMEM((64, SEQ), F32),
        ],
        compiler_params=pltpu.CompilerParams(vmem_limit_bytes=VMEM),
        cost_estimate=pl.CostEstimate(flops=9_000_000_000, bytes_accessed=10_000_000, transcendentals=1_500_000),
        name="attention_backward",
    )(y, *d_blocks, *x_blocks, qkv, o, lse, w_out, cos, sin)


def input_gradient_kernel(y_ref, a_ref, b_ref, wa_ref, wb_ref, p0, p1, p2, p3, p4):
    for start, ref in zip(_block_starts(y_ref[0]), (p0, p1, p2, p3, p4)):
        at = pl.ds(start, ref.shape[0])
        ref[...] = low(mm(a_ref[:, at].T, wa_ref[...]) + mm(b_ref[:, at].T, wb_ref[...]))


def input_gradient(y, d0, d1, w0, w1):
    smem = pl.BlockSpec(memory_space=pltpu.SMEM)
    vmem = pl.BlockSpec(memory_space=pltpu.VMEM)
    return pl.pallas_call(
        input_gradient_kernel,
        out_shape=tuple(jax.ShapeDtypeStruct((w, WIDTH), BF) for w in PIECES),
        in_specs=[smem] + [vmem] * 4,
        out_specs=[vmem] * 5,
        compiler_params=pltpu.CompilerParams(vmem_limit_bytes=VMEM),
        cost_estimate=pl.CostEstimate(flops=1_100_000_000, bytes_accessed=5_000_000, transcendentals=0),
        name="input_gradient",
    )(y, d0, d1, w0, w1)


def expert_kernel(
    slot_ref, ta, tb0, tb1, tb2, tb3, ca, cb0, cb1, cb2, cb3, pos_ref, hot_ref, wr_ref, wgu_ref, wd_ref,
    x_ref, dx_ref, act_ref, dgu_ref, dia, dib0, dib1, dib2, dib3, oa, ob0, ob1, ob2, ob3, dr_ref,
    g_scr, m_scr, y_scr, p_scr,
):
    tb, cb, dib, ob = (tb0, tb1, tb2, tb3), (cb0, cb1, cb2, cb3), (dib0, dib1, dib2, dib3), (ob0, ob1, ob2, ob3)
    place = wide(lax.broadcasted_iota(jnp.int32, (CAP, ROWS), 0))
    lane = lax.broadcasted_iota(jnp.int32, (4 * CAP, SLOTS), 1)
    for k in range(4):
        tok = jnp.concatenate([ta[0, k], tb[k][0]], axis=1)
        cot = jnp.concatenate([ca[0, k], cb[k][0]], axis=1)
        pick = jnp.concatenate([low(wide(place == pos_ref[0, k, e : e + 1, :])) for e in range(2)], axis=0)
        p_scr[k] = pick
        xs, gs, ms = low(mm(pick, tok)), low(mm(pick, cot)), mm(pick, hot_ref[0, k], NT)
        for e in range(2):
            rows = slice(k * CAP, (k + 1) * CAP)
            x_ref[e, 0, rows, :] = xs[e * CAP : (e + 1) * CAP]
            g_scr[e, rows, :] = gs[e * CAP : (e + 1) * CAP]
            m_scr[e, rows, :] = ms[e * CAP : (e + 1) * CAP]
    for e in range(2):
        x = x_ref[e, 0]
        grad = wide(g_scr[e])
        named = m_scr[e] > 0.5
        logits = jnp.where(named, mm(x, wr_ref[...]), -1e30)
        powers = jnp.where(named, jnp.exp(logits - logits.max(axis=1, keepdims=True)), 0.0)
        total = powers.sum(axis=1, keepdims=True)
        mine = jnp.where(lane == slot_ref[e], powers, 0.0).sum(axis=1, keepdims=True)
        gate = mine / jnp.where(total > 0.0, total, 1.0)
        gu = mm(x, wgu_ref[e])
        pre, up = gu[:, :FF], gu[:, FF:]
        sig = jax.nn.sigmoid(pre)
        silu = pre * sig
        act = low(silu * up)
        act_ref[e, 0] = act
        out = wide(low(mm(act, wd_ref[e])))
        d_route = (out * grad).sum(axis=1, keepdims=True)
        y_scr[0, e] = low(gate * out)
        dx = low(gate * grad)
        dx_ref[e, 0] = dx
        d_act = mm(dx, wd_ref[e], NT)
        dgu = jnp.concatenate(
            [low(d_act * up * sig * (1.0 + pre * (1.0 - sig))), low(d_act * silu)], axis=1
        )
        dgu_ref[e, 0] = dgu
        y_scr[1, e] = low(mm(dgu, wgu_ref[e], NT))
        for k in range(4):
            pick = wide(p_scr[k, e * CAP : (e + 1) * CAP, :])
            dr_ref[0, k, e : e + 1, :] = (pick * d_route[k * CAP : (k + 1) * CAP]).sum(axis=0, keepdims=True)
    for k in range(4):
        pick_t = p_scr[k].T
        for which, (a_out, b_out) in enumerate(((oa, ob[k]), (dia, dib[k]))):
            rows = jnp.concatenate([y_scr[which, e, k * CAP : (k + 1) * CAP, :] for e in range(2)], axis=0)
            dense = low(mm(pick_t, rows))
            a_out[0, k] = dense[:, :HALF]
            b_out[0] = dense[:, HALF:]


def experts(slots, tok_a, tok_b, cot_a, cot_b, pos, hot, w_router, w_gu, w_d):
    smem = pl.BlockSpec(memory_space=pltpu.SMEM)
    a_spec = pl.BlockSpec((1, 4, ROWS, HALF), lambda j: (j, 0, 0, 0))
    b_spec = pl.BlockSpec((1, ROWS, HALF), lambda j: (j, 0, 0))

    def whole(v):
        return pl.BlockSpec(v.shape, lambda j: (0,) * v.ndim, pipeline_mode=pl.Buffered(1))

    def stack(width):
        return pl.BlockSpec((2, 1, 4 * CAP, width), lambda j: (0, j, 0, 0))

    a_shape = jax.ShapeDtypeStruct((4, 4, ROWS, HALF), BF)
    b_shape = jax.ShapeDtypeStruct((4, ROWS, HALF), BF)
    return pl.pallas_call(
        expert_kernel,
        grid=(4,),
        out_shape=(
            jax.ShapeDtypeStruct((2, 4, 4 * CAP, WIDTH), BF),
            jax.ShapeDtypeStruct((2, 4, 4 * CAP, WIDTH), BF),
            jax.ShapeDtypeStruct((2, 4, 4 * CAP, FF), BF),
            jax.ShapeDtypeStruct((2, 4, 4 * CAP, 2 * FF), BF),
            a_shape, *[b_shape] * 4, a_shape, *[b_shape] * 4,
            jax.ShapeDtypeStruct((4, 4, 2, ROWS), F32),
        ),
        in_specs=[smem, a_spec, *[b_spec] * 4, a_spec, *[b_spec] * 4,
                  pl.BlockSpec((1, 4, 2, ROWS), lambda j: (j, 0, 0, 0)),
                  pl.BlockSpec((1, 4, SLOTS, ROWS), lambda j: (j, 0, 0, 0)),
                  whole(w_router), whole(w_gu), whole(w_d)],
        out_specs=[stack(WIDTH), stack(WIDTH), stack(FF), stack(2 * FF),
                   a_spec, *[b_spec] * 4, a_spec, *[b_spec] * 4,
                   pl.BlockSpec((1, 4, 2, ROWS), lambda j: (j, 0, 0, 0))],
        scratch_shapes=[
            pltpu.VMEM((2, 4 * CAP, WIDTH), BF),
            pltpu.VMEM((2, 4 * CAP, SLOTS), F32),
            pltpu.VMEM((2, 2, 4 * CAP, WIDTH), BF),
            pltpu.VMEM((4, 2 * CAP, ROWS), BF),
        ],
        compiler_params=pltpu.CompilerParams(vmem_limit_bytes=VMEM, dimension_semantics=("arbitrary",)),
        cost_estimate=pl.CostEstimate(flops=30_000_000_000, bytes_accessed=60_000_000, transcendentals=3_000_000),
        name="experts",
    )(slots, tok_a, *tok_b, cot_a, *cot_b, pos, hot, w_router, w_gu, w_d)


def expert_gradient_kernel(x_ref, dx_ref, act_ref, dgu_ref, out_ref):
    x = x_ref[0].reshape(16 * CAP, WIDTH)
    dgu = dgu_ref[0].reshape(16 * CAP, 2 * FF)
    act = act_ref[0].reshape(16 * CAP, FF)
    dx = dx_ref[0].reshape(16 * CAP, WIDTH)
    x_t = x.T
    for part in range(2):
        g = low(mm(x_t, dgu[:, part * FF : (part + 1) * FF]))
        for r in range(4):
            out_ref[r, part] = g[:, 128 * r : 128 * r + 128]
    g = low(mm(act.T, dx))
    for r in range(4):
        for k in range(8):
            out_ref[r, 2, 128 * k : 128 * k + 128, :] = g[128 * r : 128 * r + 128, 128 * k : 128 * k + 128]


def expert_gradient(e, x, dx, act, dgu):
    def stack(width):
        return pl.BlockSpec((1, 4, 4 * CAP, width), lambda i: (e, 0, 0, 0))

    return pl.pallas_call(
        expert_gradient_kernel,
        grid=(1,),
        out_shape=jax.ShapeDtypeStruct((4, 3, WIDTH, 128), BF),
        in_specs=[stack(WIDTH), stack(WIDTH), stack(FF), stack(2 * FF)],
        out_specs=pl.BlockSpec((4, 3, WIDTH, 128), lambda i: (0, 0, 0, 0)),
        compiler_params=pltpu.CompilerParams(vmem_limit_bytes=VMEM),
        cost_estimate=pl.CostEstimate(flops=4_900_000_000, bytes_accessed=14_000_000, transcendentals=0),
        name="expert_gradient",
    )(x, dx, act, dgu)


def after(value, *others):
    return lax.optimization_barrier((value, *others))[0]


def norm_scale(x):
    return lax.rsqrt(jnp.mean(x * x, axis=-1, keepdims=True) + NORM_EPS)


def shards(
    tokens, cotangent, gain_attn, w_query, w_key, w_value, w_out, gain_moe, w_router,
    w_gate, w_up, w_down, routes, owner_map,
):
    dp = lax.axis_index("dp")
    y = lax.axis_index("tensor").astype(jnp.int32).reshape(1)
    z_at, x_at, core = ring_position(dp)

    x_in = wide(tokens)
    scale_a = norm_scale(x_in)
    normed_a = low(x_in * scale_a * gain_attn)
    x_blocks = (normed_a, *gather_direct(normed_a, from_y))

    slot_ids = jnp.arange(SLOTS, dtype=jnp.int32)
    picks = routes[:, :, None] == slot_ids[None, None, :]
    route_slots = jnp.sum(jnp.where(picks, owner_map[None, None, :], 0), axis=-1)
    named = jnp.any(picks, axis=1)
    hot = low(jnp.any(route_slots.T[:, None, :] == slot_ids[None, :, None], axis=0))
    hot_z = jnp.stack([hot, from_z(hot, 1), from_z(hot, 2), from_z(hot, 3)])
    hot_all = jnp.stack([hot_z, from_x(hot_z, 1), from_x(hot_z, 2), from_x(hot_z, 3)])
    slots = jnp.stack([dp, dp + 1 - 2 * core]).astype(jnp.int32)
    mine = jnp.concatenate([lax.dynamic_slice_in_dim(hot_all, slots[e], 1, 2) for e in range(2)], axis=2)
    before = low(jnp.arange(ROWS)[:, None] < jnp.arange(ROWS)[None, :])
    rank = jnp.dot(mine.reshape(-1, ROWS), before, preferred_element_type=F32).reshape(mine.shape)
    pos = jnp.where(mine > 0, rank, -1.0)

    cot_a, cot_b = plane_gather(cotangent)

    half = HEAD // 2
    inv_freq = jnp.exp(jnp.arange(half).astype(F32) * (-2.0 * math.log(10000.0) / HEAD))
    angles = inv_freq[:, None] * jnp.arange(SEQ).astype(F32)[None, :]
    cos, sin = jnp.cos(angles), jnp.sin(angles)
    w_cat_t = jnp.concatenate([w_query, w_key, w_value], axis=1).T

    qkv, o_t, lse, *parts = attention_forward(y, x_blocks, w_cat_t, w_out, cos, sin)
    hidden = x_in + sum_direct(*parts, from_y)
    scale_m = norm_scale(hidden)
    normed_m = low(hidden * scale_m * gain_moe)

    tok_a, tok_b = plane_gather(normed_m)

    gu_own = after(jnp.concatenate([w_gate[0], w_up[0]], axis=1), normed_m)
    d_own = after(w_down[0], normed_m)
    gu_all = (gu_own, *gather_direct(gu_own, from_y))
    gu_all = (gu_all[0], gu_all[1], jnp.concatenate(gu_all[2:4], axis=0), gu_all[4])
    d_all = (d_own, *gather_direct(d_own, from_y))
    gu_full = jnp.concatenate([b[:, :128] for b in gu_all] + [b[:, 128:] for b in gu_all], axis=1)
    d_full = jnp.concatenate(d_all, axis=0)
    gu_two = jnp.stack([gu_full, from_core(gu_full)])
    d_two = jnp.stack([d_full, from_core(d_full)])
    by_slot = low(owner_map[:, None] == slot_ids[None, :])
    router_by_slot = low(jnp.dot(w_router, by_slot, preferred_element_type=F32))

    xs, dxs, acts, dgus, di_a, *rest = experts(
        slots, jnp.stack(tok_a), tok_b, jnp.stack(cot_a), cot_b, pos, hot_all, router_by_slot, gu_two, d_two
    )
    di_b, ou_a, ou_b, d_route = rest[:4], rest[4], rest[5:9], rest[9]

    by_x = [d_route[0], *[from_x(d_route[r], -r) for r in (1, 2, 3)]]
    by_x = jnp.stack(by_x)
    back = jnp.stack([by_x[:, 0], *[from_z(by_x[:, r], -r) for r in (1, 2, 3)]], axis=1)
    rel = jnp.arange(4)
    chip = ((z_at - rel[None, :]) % 4) * 4 + (x_at - rel[:, None]) % 4
    source_slots = jnp.stack([2 * chip + core, 2 * chip + 1 - core], axis=-1).reshape(-1)
    match = wide(source_slots[:, None] == owner_map[None, :])
    d_route = jnp.sum(back.reshape(SLOTS, ROWS)[:, :, None] * match[:, None, :], axis=0)

    logits = jnp.dot(normed_m, w_router, preferred_element_type=F32)
    gates = jax.nn.softmax(jnp.where(named, logits, -jnp.inf), axis=-1)
    d_logits = low(gates * (d_route - jnp.sum(gates * d_route, axis=-1, keepdims=True)))
    router_part = mm(d_logits, normed_m, TN)

    d_in = plane_sum([di_a[r] for r in range(4)], list(di_b))
    d_normed_m = mm(d_logits, w_router, NT) + d_in
    u = d_normed_m * gain_moe
    grad = wide(cotangent)
    d_hidden = grad + scale_m * u - hidden * (scale_m**3) * jnp.mean(u * hidden, axis=-1, keepdims=True)
    gain_moe_part = jnp.sum(d_normed_m * hidden * scale_m, axis=0)
    d_hidden_low = low(d_hidden)
    d_blocks = (d_hidden_low, *gather_direct(d_hidden_low, from_y))

    other = expert_gradient(1, xs, dxs, acts, dgus)
    own = expert_gradient(0, xs, dxs, acts, dgus)
    both = low(wide(own) + wide(from_core(other)))
    both = after(both, *d_blocks)
    far = jnp.concatenate(
        [from_y(both[2][:, : WIDTH // 2], 2), from_y(both[2][:, WIDTH // 2 :], -2)], axis=1
    )
    expert_sum = wide(both[0]) + wide(from_y(both[1], -1)) + wide(from_y(both[3], 1)) + wide(far)

    ou_a, *ou_b = lax.optimization_barrier((ou_a, *ou_b, d_hidden_low))[:5]
    mixed = low(hidden + plane_sum([ou_a[r] for r in range(4)], ou_b))

    out_part = out_gradient(y, d_blocks, o_t)
    dq0, gw0 = attention_backward(0, y, d_blocks, x_blocks, qkv, o_t, lse, w_out, cos, sin)
    dq1, gw1 = attention_backward(1, y, d_blocks, x_blocks, qkv, o_t, lse, w_out, cos, sin)
    w0 = jnp.concatenate([w_cat_t[:128], w_cat_t[256:320], w_cat_t[384:448]], axis=0)
    w1 = jnp.concatenate([w_cat_t[128:256], w_cat_t[320:384], w_cat_t[448:]], axis=0)
    d_parts = input_gradient(y, dq0, dq1, w0, w1)
    d_normed_a = sum_direct(*d_parts, from_y)
    u = d_normed_a * gain_attn
    d_tokens = d_hidden + scale_a * u - x_in * (scale_a**3) * jnp.mean(u * x_in, axis=-1, keepdims=True)

    small = jnp.concatenate([router_part, gain_moe_part[None, :], jnp.zeros((31, WIDTH), F32)], axis=0)
    small = tensor_sum(small)
    bundle = dp_sum(jnp.concatenate([out_part, low(small)], axis=0), dp)
    g_out = wide(bundle[:256])
    g_router = wide(bundle[256:288]).T
    g_gain_moe = wide(bundle[288])
    gw = dp_sum(jnp.concatenate([gw0, gw1], axis=0), dp)
    gw_wide = wide(gw)
    rows = jnp.sum(gw_wide * wide(jnp.concatenate([w0, w1], axis=0)), axis=0)
    g_gain_attn = tensor_sum(rows) / gain_attn
    g_query = jnp.concatenate([gw_wide[:128], gw_wide[256:384]], axis=0).T
    g_key = jnp.concatenate([gw_wide[128:192], gw_wide[384:448]], axis=0).T
    g_value = jnp.concatenate([gw_wide[192:256], gw_wide[448:]], axis=0).T
    g_down = expert_sum[2].reshape(8, 128, 128).transpose(1, 0, 2).reshape(1, 128, WIDTH)
    return (
        mixed, d_tokens, g_gain_attn, g_query, g_key, g_value, g_out, g_gain_moe, g_router,
        expert_sum[0][None], expert_sum[1][None], g_down,
    )


def solution(mesh):
    both = P(("dp", "tensor"), None)
    in_specs = (
        both, both, P(), P(None, "tensor"), P(None, "tensor"), P(None, "tensor"), P("tensor", None), P(), P(),
        P("dp", None, "tensor"), P("dp", None, "tensor"), P("dp", "tensor", None), both, P(),
    )
    out_specs = (
        both, both, P(), P(None, "tensor"), P(None, "tensor"), P(None, "tensor"), P("tensor", None), P(), P(),
        P("dp", None, "tensor"), P("dp", None, "tensor"), P("dp", "tensor", None),
    )
    return jax.shard_map(shards, mesh=mesh, in_specs=in_specs, out_specs=out_specs, check_vma=False)
```

time: 1030 us -> 591 us (0.57); the launches traced: 1010 us -> 584 us
  matrix products: 210 us -> 2.08 us
  waiting for transfers between devices: 402 us -> 219 us
  blocking collectives: 143 us -> 0 us
  starting transfers between devices: 48.2 us -> 173 us
  local copies, waits for them, and re-layouts: 129 us -> 23.5 us
  Pallas kernels: 0 us -> 102 us
  between operations: 15 us -> 2.9 us
  loops' own time: 11.3 us -> 0 us
    ppermute x0 -> x141, waiting for transfers between devices: none -> 219 us  [the longest x54 87.6 us: from_x(): return lax.ppermute(v, 'dp', _dp_pairs(0, d, 0))]
    dot_general x40 -> x5, matrix products: 210 us -> 2.08 us  [the longest x1 0.8 us: shards(): jnp.dot(mine.reshape(-1, ROWS), before, preferred_element_type=F32)]
    all_to_all x7 -> x0, waiting for transfers between devices: 196 us -> none  [the longest x1 72.3 us: shards(): lax.all_to_all(out_rows_low, 'dp', split_axis=0, concat_axis=0, tiled=True)]
    ppermute x0 -> x141, starting transfers between devices: none -> 173 us  [the longest x46 65.1 us: from_z(): return lax.ppermute(v, 'dp', _dp_pairs(d, 0, 0))]
    psum x2 -> x0, waiting for transfers between devices: 162 us -> none  [the longest x1 94.9 us: shards(): lax.psum(query_grad.astype(jnp.bfloat16), 'dp').astype(jnp.float32)]
    pallas_call x0 -> x8, Pallas kernels: none -> 102 us  [the longest x1 43.5 us: experts(): pl.pallas_call(expert_kernel, grid=(4,), out_shape=(jax.ShapeDtypeStruct(...]
    all_to_all x1 -> x0, blocking collectives: 79.8 us -> none  [shards(): lax.all_to_all(send_grads, 'dp', split_axis=0, concat_axis=0, tiled=True)]
    psum x1 -> x0, blocking collectives: 63.4 us -> none  [shards(): lax.psum((gain_attn_part, gain_moe_part, router_part), ('dp', 'tensor'))]
  transfers between devices with their start and end apart: 12 -> 141, of which waited for: 9 -> 53; matrix products, arithmetic and copies ran while one was open for 24% -> 13% of each run, Pallas kernels for 0% -> 6%
where the time goes in v1:
time: 591 us; the launch traced here: 584 us
  waiting for transfers between devices  219 us (37%)
  starting transfers between devices  173 us (29%)
  Pallas kernels  102 us (17%)
  other arithmetic  61.4 us (10%)
  local copies, waits for them, and re-layouts  23.5 us (4%)
    ppermute x54, waiting for transfers between devices, from_x(): return lax.ppermute(v, 'dp', _dp_pairs(0, d, 0))  87.6 us
    ppermute x34, waiting for transfers between devices, from_y(): return lax.ppermute(v, 'tensor', [((i + d) % 4, i) for i in range(4)])  68 us
    ppermute x46, starting transfers between devices, from_z(): return lax.ppermute(v, 'dp', _dp_pairs(d, 0, 0))  65.1 us
    ppermute x54, starting transfers between devices, from_x(): return lax.ppermute(v, 'dp', _dp_pairs(0, d, 0))  62.7 us
    ppermute x46, waiting for transfers between devices, from_z(): return lax.ppermute(v, 'dp', _dp_pairs(d, 0, 0))  62.2 us
    ppermute x34, starting transfers between devices, from_y(): return lax.ppermute(v, 'tensor', [((i + d) % 4, i) for i in range(4)])  44.8 us
    pallas_call x1, Pallas kernels, experts(): pl.pallas_call(expert_kernel, grid=(4,), out_shape=(jax.ShapeDtypeStruct(...  43.5 us
    pallas_call x2, Pallas kernels, expert_gradient(): pl.pallas_call(expert_gradient_kernel, grid=(1,), out_shape=jax.ShapeDtyp...  21.9 us
  transfers between devices with their start and end apart: 141, of which 53 were waited for; matrix products, arithmetic and copies ran while one was open for 13% of the time, Pallas kernels for 6%

profile of v1, /device:TPU:14, one launch (start us, length us, event | category | flops | bytes accessed | tf_op | source)
XLA Modules:
  0.0 584.2 jit_solution(11691338564674518987)
XLA Ops:
  7.5 4.0 collective-permute-start.40
  39.6 10.2 %attention_forward.1 = (bf16[512,1024]{1,0:T(8,128)(2,1)}, f32[256,1024]{1,0:T(8,128)}, f32[8,1024]{1,0:T(8,128)}, bf16[256,1024]{1,0:T(8,128)(2,1)}, bf16[256,1...) custom-call(s32[1]{0:T(128)} %bitcast.y_ref, ...), custom_call_target="tpu_custom_call" | custom-call | flops 8000000000 | bytes 10000000 | tf_op jit(solution)/shard_map/attention_forward/pallas_call | solution.py:219
  62.9 9.7 %collective-permute-done.6 = bf16[128,1024]{1,0:T(8,128)(2,1)S(1)} collective-permute-done((bf16[128,1024]{1,0:T(8,128)(2,1)}, bf16[128,1024]{1,0:T(8,128)(2,1)S(1)}, u32[]{:S(2)}, u32[]{:S(2)}) %collective-permute-start.6) | collective-permute-done | bytes 262176 | tf_op jit(solution)/shard_map/ppermute | solution.py:56
  105.6 3.8 collective-permute-start.19
  112.8 8.4 %collective-permute-done.17 = bf16[1,128,512]{2,1,0:T(8,128)(2,1)S(1)} collective-permute-done((bf16[1,128,512]{2,1,0:T(8,128)(2,1)S(1)}, bf16[1,128,512]{2,1,0:T(8,128)(2,1)S(1)}, u32[]{:S(2)}, u32[]{:S(2)}) %collective-permute-start.17) | collective-permute-done | bytes 131104 | tf_op jit(solution)/shard_map/ppermute | solution.py:48
  121.8 3.7 collective-permute-done.19
  135.9 5.4 collective-permute-done.49
  143.4 11.0 %collective-permute-done.36.cb1 = bf16[4,256,512]{2,1,0:T(8,128)(2,1)S(1)} collective-permute-done((bf16[4,256,512]{2,1,0:T(8,128)(2,1)S(1)}, bf16[4,256,512]{2,1,0:T(8,128)(2,1)S(1)}, u32[]{:S(2)}, u32[]{:S(2)}) %collective-permute-start.36) | collective-permute-done | bytes 1048608 | tf_op jit(solution)/shard_map/ppermute | solution.py:44
  158.7 13.4 %collective-permute-done.20.tb1 = bf16[4,256,512]{2,1,0:T(8,128)(2,1)S(1)} collective-permute-done((bf16[4,256,512]{2,1,0:T(8,128)(2,1)S(1)}, bf16[4,256,512]{2,1,0:T(8,128)(2,1)S(1)}, u32[]{:S(2)}, u32[]{:S(2)}) %collective-permute-start.20) | collective-permute-done | bytes 1048608 | tf_op jit(solution)/shard_map/ppermute | solution.py:44
  177.0 4.5 collective-permute-done.14
  184.3 4.9 collective-permute-done.37
  208.7 43.5 %experts.1 = (bf16[2,4,384,1024]{3,2,1,0:T(8,128)(2,1)}, bf16[2,4,384,1024]{3,2,1,0:T(8,128)(2,1)}, bf16[2,4,384,512]{3,2,1,0:T(8,128)(2,1)}, bf16[2,4,384,1024]...) custom-call(s32[2]{0:T(128)} %pad_add_fusion.1.slot_ref, ...), custom_call_target="tpu_custom_call" | custom-call | flops 30000001024 | bytes 60000000 | tf_op jit(solution)/shard_map/experts/pallas_call | solution.py:428
  252.3 10.9 %expert_gradient.2 = bf16[4,3,1024,128]{3,2,1,0:T(8,128)(2,1)} custom-call(bf16[2,4,384,1024]{3,2,1,0:T(8,128)(2,1)} %get-tuple-element.87.x_ref, bf16[2,4,384,1024]{3,2,1,0:T(8,128)(2,1)} %get-tuple-element.88.dx_ref, bf16[2,4,384,512]{3,2,1,0:T(8,128)(2,1)} %get-tuple-element.89.act_ref, bf16[2,4,384,1024]{3,2,1,0:T(8,128)(2,1)} %get-tuple-element.90.dgu_ref), custom_call_target="tpu_custom_call" | custom-call | flops 4899999744 | bytes 14000000 | tf_op jit(solution)/shard_map/expert_gradient/pallas_call | solution.py:478
  263.2 10.9 %expert_gradient.3 = bf16[4,3,1024,128]{3,2,1,0:T(8,128)(2,1)} custom-call(bf16[2,4,384,1024]{3,2,1,0:T(8,128)(2,1)} %get-tuple-element.87.x_ref, bf16[2,4,384,1024]{3,2,1,0:T(8,128)(2,1)} %get-tuple-element.88.dx_ref, bf16[2,4,384,512]{3,2,1,0:T(8,128)(2,1)} %get-tuple-element.89.act_ref, bf16[2,4,384,1024]{3,2,1,0:T(8,128)(2,1)} %get-tuple-element.90.dgu_ref), custom_call_target="tpu_custom_call" | custom-call | flops 4899999744 | bytes 14000000 | tf_op jit(solution)/shard_map/expert_gradient/pallas_call | solution.py:478
  286.4 5.1 collective-permute-done.62
  306.0 11.8 %collective-permute-done.63 = bf16[4,256,512]{2,1,0:T(8,128)(2,1)} collective-permute-done((bf16[4,256,512]{2,1,0:T(8,128)(2,1)}, bf16[4,256,512]{2,1,0:T(8,128)(2,1)}, u32[]{:S(2)}, u32[]{:S(2)}) %collective-permute-start.63) | collective-permute-done | bytes 1048608 | tf_op jit(solution)/shard_map/ppermute | solution.py:48
  339.2 3.7 collective-permute-done.75
  351.9 14.6 %collective-permute-done.119 = f32[64,1024]{1,0:T(8,128)S(1)} collective-permute-done((f32[64,1024]{1,0:T(8,128)S(1)}, f32[64,1024]{1,0:T(8,128)S(1)}, u32[]{:S(2)}, u32[]{:S(2)}) %collective-permute-start.119) | collective-permute-done | bytes 262176 | tf_op jit(solution)/shard_map/ppermute | solution.py:56
  388.4 9.8 %attention_backward.3 = (bf16[256,1024]{1,0:T(8,128)(2,1)}, bf16[256,1024]{1,0:T(8,128)(2,1)}) custom-call(s32[1]{0:T(128)} %bitcast.y_ref, bf16[256,1024]{1,0:T(8,128)(2,1)} %copy-done.4, bf16[256,1024]{1,0:T(8,128)(2,1)} %copy-done.41, bf16[128,1024]{1,0:T(8,128)(2,1)} %copy-done.54, bf16[128,1024]{1,0:T(8,128)(2,1)} %copy-done.55, ...), custom_call_target="tpu_custom_call" | custom-call | flops 8999999488 | bytes 10000000 | tf_op jit(solution)/shard_map/attention_backward/pallas_call | solution.py:318
  398.2 9.8 %attention_backward.2 = (bf16[256,1024]{1,0:T(8,128)(2,1)}, bf16[256,1024]{1,0:T(8,128)(2,1)}) custom-call(s32[1]{0:T(128)} %bitcast.y_ref, bf16[256,1024]{1,0:T(8,128)(2,1)} %copy-done.4, bf16[256,1024]{1,0:T(8,128)(2,1)} %copy-done.41, bf16[128,1024]{1,0:T(8,128)(2,1)} %copy-done.54, bf16[128,1024]{1,0:T(8,128)(2,1)} %copy-done.55, ...), custom_call_target="tpu_custom_call" | custom-call | flops 8999999488 | bytes 10000000 | tf_op jit(solution)/shard_map/attention_backward/pallas_call | solution.py:318
  422.5 3.7 input_gradient.1
  437.3 4.7 collective-permute-done.128
  444.8 9.6 %collective-permute-done.100 = bf16[128,1024]{1,0:T(8,128)(2,1)S(1)} collective-permute-done((bf16[128,1024]{1,0:T(8,128)(2,1)}, bf16[128,1024]{1,0:T(8,128)(2,1)S(1)}, u32[]{:S(2)}, u32[]{:S(2)}) %collective-permute-start.100) | collective-permute-done | bytes 262176 | tf_op jit(solution)/shard_map/ppermute | solution.py:56
  473.4 3.6 concatenate.241
  481.7 3.7 add_convert_fusion
  500.6 14.8 %collective-permute-done.111 = bf16[64,1024]{1,0:T(8,128)(2,1)S(1)} collective-permute-done((bf16[64,1024]{1,0:T(8,128)(2,1)S(1)}, bf16[64,1024]{1,0:T(8,128)(2,1)S(1)}, u32[]{:S(2)}, u32[]{:S(2)}) %collective-permute-start.111) | collective-permute-done | bytes 131104 | tf_op jit(solution)/shard_map/ppermute | solution.py:48
  515.4 5.8 collective-permute-done.112
  521.1 5.8 collective-permute-done.113
  534.7 9.1 %collective-permute-done.89 = bf16[4,256,512]{2,1,0:T(8,128)(2,1)S(1)} collective-permute-done((bf16[4,256,512]{2,1,0:T(8,128)(2,1)S(1)}, bf16[4,256,512]{2,1,0:T(8,128)(2,1)S(1)}, u32[]{:S(2)}, u32[]{:S(2)}) %collective-permute-start.89) | collective-permute-done | bytes 1048608 | tf_op jit(solution)/shard_map/ppermute | solution.py:44
  543.8 3.7 collective-permute-start.84
  557.1 3.7 collective-permute-start.85
  560.8 4.2 collective-permute-done.137
  (612 shorter events, 310.1 us)
Async XLA Ops:
  3.9 31.1 %collective-permute-start = (bf16[256,1024]{1,0:T(8,128)(2,1)S(1)}, bf16[256,1024]{1,0:T(8,128)(2,1)}, u32[]{:S(2)}, u32[]{:S(2)}) collective-permute-start(bf16[256,1024]{1,0:T(8,128)(2,1)S(1)} %fusion.8.n0.x0), channel_id=1, source_target_pairs={{1,0},{2,1},{3,2},{0,3},{5,4},{6,5},{7,6},{4,7},{9,8},{10,9},{11,1... | collective-permute-start | bytes 1572872 | tf_op jit(solution)/shard_map/ppermute | solution.py:56
  4.4 33.0 %collective-permute-start.3 = (bf16[256,1024]{1,0:T(8,128)(2,1)S(1)}, bf16[256,1024]{1,0:T(8,128)(2,1)}, u32[]{:S(2)}, u32[]{:S(2)}) collective-permute-start(bf16[256,1024]{1,0:T(8,128)(2,1)S(1)} %fusion.8.n0.x0), channel_id=1, source_target_pairs={{3,0},{0,1},{1,2},{2,3},{7,4},{4,5},{5,6},{6,7},{11,8},{8,9},{9,10... | collective-permute-start | bytes 1572872 | tf_op jit(solution)/shard_map/ppermute | solution.py:56
  31.5 24.4 %collective-permute-start.32 = (bf16[1,256,512]{2,1,0:T(8,128)(2,1)S(1)}, bf16[1,256,512]{2,1,0:T(8,128)(2,1)S(1)}, u32[]{:S(2)}, u32[]{:S(2)}) collective-permute-start(bf16[1,256,512]{2,1,0:T(8,128)(2,1)S(1)} %get-tuple-element.218), channel_id=1, source_target_pairs={{8,0},{12,4},{16,8},{20,12},{24,16},{28,20},{0,24},{4,28},{40,32},... | collective-permute-start | bytes 786440 | tf_op jit(solution)/shard_map/ppermute | solution.py:48
  34.5 22.7 %collective-permute-start.34 = (bf16[1,256,512]{2,1,0:T(8,128)(2,1)S(1)}, bf16[1,256,512]{2,1,0:T(8,128)(2,1)}, u32[]{:S(2)}, u32[]{:S(2)}) collective-permute-start(bf16[1,256,512]{2,1,0:T(8,128)(2,1)S(1)} %get-tuple-element.218), channel_id=1, source_target_pairs={{24,0},{28,4},{0,8},{4,12},{8,16},{12,20},{16,24},{20,28},{56,32},... | collective-permute-start | bytes 786440 | tf_op jit(solution)/shard_map/ppermute | solution.py:48
  50.7 24.8 %collective-permute-start.4 = (bf16[256,1024]{1,0:T(8,128)(2,1)}, bf16[256,1024]{1,0:T(8,128)(2,1)}, u32[]{:S(2)}, u32[]{:S(2)}) collective-permute-start(bf16[256,1024]{1,0:T(8,128)(2,1)} %get-tuple-element.53), channel_id=1, source_target_pairs={{3,0},{0,1},{1,2},{2,3},{7,4},{4,5},{5,6},{6,7},{11,8},{8,9},{9,10... | collective-permute-start | bytes 1572872 | tf_op jit(solution)/shard_map/ppermute | solution.py:56
  52.1 23.5 %collective-permute-start.5 = (bf16[256,1024]{1,0:T(8,128)(2,1)}, bf16[256,1024]{1,0:T(8,128)(2,1)}, u32[]{:S(2)}, u32[]{:S(2)}) collective-permute-start(bf16[256,1024]{1,0:T(8,128)(2,1)} %get-tuple-element.54), channel_id=1, source_target_pairs={{1,0},{2,1},{3,2},{0,3},{5,4},{6,5},{7,6},{4,7},{9,8},{10,9},{11,1... | collective-permute-start | bytes 1572872 | tf_op jit(solution)/shard_map/ppermute | solution.py:56
  93.8 38.3 %collective-permute-start.28 = (bf16[4,256,512]{2,1,0:T(8,128)(2,1)S(1)}, bf16[4,256,512]{2,1,0:T(8,128)(2,1)S(1)}, u32[]{:S(2)}, u32[]{:S(2)}) collective-permute-start(bf16[4,256,512]{2,1,0:T(8,128)(2,1)S(1)} %pad_maximum_fusion.7), channel_id=1, source_target_pairs={{8,0},{12,4},{16,8},{20,12},{24,16},{28,20},{0,24},{4,28},{40,32},... | collective-permute-start | bytes 3145736 | tf_op jit(solution)/shard_map/ppermute | solution.py:48
  100.4 31.9 %collective-permute-start.30 = (bf16[4,256,512]{2,1,0:T(8,128)(2,1)S(1)}, bf16[4,256,512]{2,1,0:T(8,128)(2,1)S(1)}, u32[]{:S(2)}, u32[]{:S(2)}) collective-permute-start(bf16[4,256,512]{2,1,0:T(8,128)(2,1)S(1)} %pad_maximum_fusion.7), channel_id=1, source_target_pairs={{24,0},{28,4},{0,8},{4,12},{8,16},{12,20},{16,24},{20,28},{56,32},... | collective-permute-start | bytes 3145736 | tf_op jit(solution)/shard_map/ppermute | solution.py:48
  112.4 23.2 %collective-permute-start.46 = (bf16[1024,256]{1,0:T(8,128)(2,1)S(1)}, bf16[1024,256]{1,0:T(8,128)(2,1)S(1)}, u32[]{:S(2)}, u32[]{:S(2)}) collective-permute-start(bf16[1024,256]{1,0:T(8,128)(2,1)S(1)} %pad_maximum_fusion.18), channel_id=1, source_target_pairs={{1,0},{2,1},{3,2},{0,3},{5,4},{6,5},{7,6},{4,7},{9,8},{10,9},{11,1... | collective-permute-start | bytes 1572872 | tf_op jit(solution)/shard_map/ppermute | solution.py:56
  127.4 27.0 %collective-permute-start.36 = (bf16[4,256,512]{2,1,0:T(8,128)(2,1)S(1)}, bf16[4,256,512]{2,1,0:T(8,128)(2,1)S(1)}, u32[]{:S(2)}, u32[]{:S(2)}) collective-permute-start(bf16[4,256,512]{2,1,0:T(8,128)(2,1)S(1)} %pad_maximum_fusion.8.cb0), channel_id=1, source_target_pairs={{32,0},{36,4},{40,8},{44,12},{48,16},{52,20},{56,24},{60,28},{64,3... | collective-permute-start | bytes 3145736 | tf_op jit(solution)/shard_map/ppermute | solution.py:44
  131.9 23.0 %collective-permute-start.38 = (bf16[4,256,512]{2,1,0:T(8,128)(2,1)S(1)}, bf16[4,256,512]{2,1,0:T(8,128)(2,1)S(1)}, u32[]{:S(2)}, u32[]{:S(2)}) collective-permute-start(bf16[4,256,512]{2,1,0:T(8,128)(2,1)S(1)} %pad_maximum_fusion.8.cb0), channel_id=1, source_target_pairs={{96,0},{100,4},{104,8},{108,12},{112,16},{116,20},{120,24},{124,28... | collective-permute-start | bytes 3145736 | tf_op jit(solution)/shard_map/ppermute | solution.py:44
  132.3 39.8 %collective-permute-start.20 = (bf16[4,256,512]{2,1,0:T(8,128)(2,1)S(1)}, bf16[4,256,512]{2,1,0:T(8,128)(2,1)S(1)}, u32[]{:S(2)}, u32[]{:S(2)}) collective-permute-start(bf16[4,256,512]{2,1,0:T(8,128)(2,1)S(1)} %pad_maximum_fusion.5.tb0), channel_id=1, source_target_pairs={{32,0},{36,4},{40,8},{44,12},{48,16},{52,20},{56,24},{60,28},{64,3... | collective-permute-start | bytes 3145736 | tf_op jit(solution)/shard_map/ppermute | solution.py:44
  155.2 35.1 %collective-permute-start.55 = (bf16[512,1024]{1,0:T(8,128)(2,1)S(1)}, bf16[512,1024]{1,0:T(8,128)(2,1)S(1)}, u32[]{:S(2)}, u32[]{:S(2)}) collective-permute-start(bf16[512,1024]{1,0:T(8,128)(2,1)S(1)} %constant_dynamic-update-slice_fusion.2), channel_id=1, source_target_pairs={{4,0},{0,4},{12,8},{8,12},{20,16},{16,20},{28,24},{24,28},{36,32},... | collective-permute-start | bytes 3145736 | tf_op jit(solution)/shard_map/ppermute | solution.py:52
  155.3 26.2 %collective-permute-start.14 = (bf16[4,256,512]{2,1,0:T(8,128)(2,1)S(1)}, bf16[4,256,512]{2,1,0:T(8,128)(2,1)S(1)}, u32[]{:S(2)}, u32[]{:S(2)}) collective-permute-start(bf16[4,256,512]{2,1,0:T(8,128)(2,1)S(1)} %pad_maximum_fusion.4), channel_id=1, source_target_pairs={{24,0},{28,4},{0,8},{4,12},{8,16},{12,20},{16,24},{20,28},{56,32},... | collective-permute-start | bytes 3145736 | tf_op jit(solution)/shard_map/ppermute | solution.py:48
  172.1 34.3 %collective-permute-start.50 = (bf16[1024,1024]{1,0:T(8,128)(2,1)S(1)}, bf16[1024,1024]{1,0:T(8,128)(2,1)S(1)}, u32[]{:S(2)}, u32[]{:S(2)}) collective-permute-start(bf16[1024,1024]{1,0:T(8,128)(2,1)S(1)} %slice_dynamic-update-slice_fusion), channel_id=1, source_target_pairs={{4,0},{0,4},{12,8},{8,12},{20,16},{16,20},{28,24},{24,28},{36,32},... | collective-permute-start | bytes 6291464 | tf_op jit(solution)/shard_map/ppermute | solution.py:52
  302.5 23.7 %collective-permute-start.71 = (bf16[4,256,512]{2,1,0:T(8,128)(2,1)}, bf16[4,256,512]{2,1,0:T(8,128)(2,1)}, u32[]{:S(2)}, u32[]{:S(2)}) collective-permute-start(bf16[4,256,512]{2,1,0:T(8,128)(2,1)} %pad_maximum_fusion.12), channel_id=1, source_target_pairs={{96,0},{100,4},{104,8},{108,12},{112,16},{116,20},{120,24},{124,28... | collective-permute-start | bytes 3145736 | tf_op jit(solution)/shard_map/ppermute | solution.py:44
  345.9 32.4 %collective-permute-start.94 = (bf16[256,1024]{1,0:T(8,128)(2,1)S(1)}, bf16[256,1024]{1,0:T(8,128)(2,1)S(1)}, u32[]{:S(2)}, u32[]{:S(2)}) collective-permute-start(bf16[256,1024]{1,0:T(8,128)(2,1)S(1)} %get-tuple-element.144.d0), channel_id=1, source_target_pairs={{1,0},{2,1},{3,2},{0,3},{5,4},{6,5},{7,6},{4,7},{9,8},{10,9},{11,1... | collective-permute-start | bytes 1572872 | tf_op jit(solution)/shard_map/ppermute | solution.py:56
  345.9 34.2 %collective-permute-start.97 = (bf16[256,1024]{1,0:T(8,128)(2,1)S(1)}, bf16[256,1024]{1,0:T(8,128)(2,1)S(1)}, u32[]{:S(2)}, u32[]{:S(2)}) collective-permute-start(bf16[256,1024]{1,0:T(8,128)(2,1)S(1)} %get-tuple-element.144.d0), channel_id=1, source_target_pairs={{3,0},{0,1},{1,2},{2,3},{7,4},{4,5},{5,6},{6,7},{11,8},{8,9},{9,10... | collective-permute-start | bytes 1572872 | tf_op jit(solution)/shard_map/ppermute | solution.py:56
  371.2 110.5 %collective-permute-start.136 = (bf16[4,3,1024,128]{3,2,1,0:T(8,128)(2,1)}, bf16[4,3,1024,128]{3,2,1,0:T(8,128)(2,1)}, u32[]{:S(2)}, u32[]{:S(2)}) collective-permute-start(bf16[4,3,1024,128]{3,2,1,0:T(8,128)(2,1)} %expert_gradient.3), channel_id=1, source_target_pairs={{4,0},{0,4},{12,8},{8,12},{20,16},{16,20},{28,24},{24,28},{36,32},... | collective-permute-start | bytes 9437192 | tf_op jit(solution)/shard_map/ppermute | solution.py:52
  374.4 33.6 %collective-permute-start.78 = (bf16[2,256,512]{2,1,0:T(8,128)(2,1)}, bf16[2,256,512]{2,1,0:T(8,128)(2,1)}, u32[]{:S(2)}, u32[]{:S(2)}) collective-permute-start(bf16[2,256,512]{2,1,0:T(8,128)(2,1)} %get-tuple-element.150), channel_id=1, source_target_pairs={{24,0},{28,4},{0,8},{4,12},{8,16},{12,20},{16,24},{20,28},{56,32},... | collective-permute-start | bytes 1572872 | tf_op jit(solution)/shard_map/ppermute | solution.py:48
  377.2 30.9 %collective-permute-start.80 = (bf16[2,256,512]{2,1,0:T(8,128)(2,1)}, bf16[2,256,512]{2,1,0:T(8,128)(2,1)}, u32[]{:S(2)}, u32[]{:S(2)}) collective-permute-start(bf16[2,256,512]{2,1,0:T(8,128)(2,1)} %get-tuple-element.151), channel_id=1, source_target_pairs={{8,0},{12,4},{16,8},{20,12},{24,16},{28,20},{0,24},{4,28},{40,32},... | collective-permute-start | bytes 1572872 | tf_op jit(solution)/shard_map/ppermute | solution.py:48
  378.2 33.8 %collective-permute-start.86 = (bf16[2,256,512]{2,1,0:T(8,128)(2,1)}, bf16[2,256,512]{2,1,0:T(8,128)(2,1)S(1)}, u32[]{:S(2)}, u32[]{:S(2)}) collective-permute-start(bf16[2,256,512]{2,1,0:T(8,128)(2,1)} %get-tuple-element.192), channel_id=1, source_target_pairs={{96,0},{100,4},{104,8},{108,12},{112,16},{116,20},{120,24},{124,28... | collective-permute-start | bytes 1572872 | tf_op jit(solution)/shard_map/ppermute | solution.py:44
  380.9 31.2 %collective-permute-start.88 = (bf16[2,256,512]{2,1,0:T(8,128)(2,1)}, bf16[2,256,512]{2,1,0:T(8,128)(2,1)}, u32[]{:S(2)}, u32[]{:S(2)}) collective-permute-start(bf16[2,256,512]{2,1,0:T(8,128)(2,1)} %get-tuple-element.193), channel_id=1, source_target_pairs={{32,0},{36,4},{40,8},{44,12},{48,16},{52,20},{56,24},{60,28},{64,3... | collective-permute-start | bytes 1572872 | tf_op jit(solution)/shard_map/ppermute | solution.py:44
  426.2 31.3 %collective-permute-start.98 = (bf16[256,1024]{1,0:T(8,128)(2,1)}, bf16[256,1024]{1,0:T(8,128)(2,1)S(1)}, u32[]{:S(2)}, u32[]{:S(2)}) collective-permute-start(bf16[256,1024]{1,0:T(8,128)(2,1)} %get-tuple-element.81), channel_id=1, source_target_pairs={{3,0},{0,1},{1,2},{2,3},{7,4},{4,5},{5,6},{6,7},{11,8},{8,9},{9,10... | collective-permute-start | bytes 1572872 | tf_op jit(solution)/shard_map/ppermute | solution.py:56
  435.0 25.4 %collective-permute-start.99 = (bf16[256,1024]{1,0:T(8,128)(2,1)}, bf16[256,1024]{1,0:T(8,128)(2,1)S(1)}, u32[]{:S(2)}, u32[]{:S(2)}) collective-permute-start(bf16[256,1024]{1,0:T(8,128)(2,1)} %get-tuple-element.82), channel_id=1, source_target_pairs={{1,0},{2,1},{3,2},{0,3},{5,4},{6,5},{7,6},{4,7},{9,8},{10,9},{11,1... | collective-permute-start | bytes 1572872 | tf_op jit(solution)/shard_map/ppermute | solution.py:56
  477.0 55.1 %collective-permute-start.79 = (bf16[4,256,512]{2,1,0:T(8,128)(2,1)}, bf16[4,256,512]{2,1,0:T(8,128)(2,1)S(1)}, u32[]{:S(2)}, u32[]{:S(2)}) collective-permute-start(bf16[4,256,512]{2,1,0:T(8,128)(2,1)} %pad_maximum_fusion.14), channel_id=1, source_target_pairs={{24,0},{28,4},{0,8},{4,12},{8,16},{12,20},{16,24},{20,28},{56,32},... | collective-permute-start | bytes 3145736 | tf_op jit(solution)/shard_map/ppermute | solution.py:48
  492.2 40.8 %collective-permute-start.81 = (bf16[4,256,512]{2,1,0:T(8,128)(2,1)S(1)}, bf16[4,256,512]{2,1,0:T(8,128)(2,1)S(1)}, u32[]{:S(2)}, u32[]{:S(2)}) collective-permute-start(bf16[4,256,512]{2,1,0:T(8,128)(2,1)S(1)} %copy-done.22), channel_id=1, source_target_pairs={{8,0},{12,4},{16,8},{20,12},{24,16},{28,20},{0,24},{4,28},{40,32},... | collective-permute-start | bytes 3145736 | tf_op jit(solution)/shard_map/ppermute | solution.py:48
  493.6 41.1 %collective-permute-start.87 = (bf16[4,256,512]{2,1,0:T(8,128)(2,1)S(1)}, bf16[4,256,512]{2,1,0:T(8,128)(2,1)S(1)}, u32[]{:S(2)}, u32[]{:S(2)}) collective-permute-start(bf16[4,256,512]{2,1,0:T(8,128)(2,1)S(1)} %copy-done.23), channel_id=1, source_target_pairs={{96,0},{100,4},{104,8},{108,12},{112,16},{116,20},{120,24},{124,28... | collective-permute-start | bytes 3145736 | tf_op jit(solution)/shard_map/ppermute | solution.py:44
  496.2 32.9 %collective-permute-start.114 = (bf16[64,1024]{1,0:T(8,128)(2,1)S(1)}, bf16[64,1024]{1,0:T(8,128)(2,1)S(1)}, u32[]{:S(2)}, u32[]{:S(2)}) collective-permute-start(bf16[64,1024]{1,0:T(8,128)(2,1)S(1)} %get-tuple-element.143), channel_id=1, source_target_pairs={{24,0},{28,4},{0,8},{4,12},{8,16},{12,20},{16,24},{20,28},{56,32},... | collective-permute-start | bytes 393224 | tf_op jit(solution)/shard_map/ppermute | solution.py:48
  529.1 28.0 %collective-permute-start.139 = (bf16[3,512,128]{2,1,0:T(8,128)(2,1)S(1)}, bf16[3,512,128]{2,1,0:T(8,128)(2,1)S(1)}, u32[]{:S(2)}, u32[]{:S(2)}) collective-permute-start(bf16[3,512,128]{2,1,0:T(8,128)(2,1)S(1)} %get-tuple-element.208), channel_id=1, source_target_pairs={{2,0},{3,1},{0,2},{1,3},{6,4},{7,5},{4,6},{5,7},{10,8},{11,9},{8,1... | collective-permute-start | bytes 1179656 | tf_op jit(solution)/shard_map/ppermute | solution.py:56
  532.1 28.7 %collective-permute-start.140 = (bf16[3,512,128]{2,1,0:T(8,128)(2,1)S(1)}, bf16[3,512,128]{2,1,0:T(8,128)(2,1)S(1)}, u32[]{:S(2)}, u32[]{:S(2)}) collective-permute-start(bf16[3,512,128]{2,1,0:T(8,128)(2,1)S(1)} %get-tuple-element.209), channel_id=1, source_target_pairs={{2,0},{3,1},{0,2},{1,3},{6,4},{7,5},{4,6},{5,7},{10,8},{11,9},{8,1... | collective-permute-start | bytes 1179656 | tf_op jit(solution)/shard_map/ppermute | solution.py:56
  532.9 23.4 %collective-permute-start.115 = (bf16[256,1024]{1,0:T(8,128)(2,1)S(1)}, bf16[256,1024]{1,0:T(8,128)(2,1)S(1)}, u32[]{:S(2)}, u32[]{:S(2)}) collective-permute-start(bf16[256,1024]{1,0:T(8,128)(2,1)S(1)} %constant_dynamic-slice_fusion.6), channel_id=1, source_target_pairs={{4,0},{0,4},{12,8},{8,12},{20,16},{16,20},{28,24},{24,28},{36,32},... | collective-permute-start | bytes 1572872 | tf_op jit(solution)/shard_map/ppermute | solution.py:52
  (181 other events, 2177.4 us)
